TPU v7x, 32 devices: a whole 2x2x4 slice. The times are simulated.
32 devices in a mesh: box: 4 (over x, core), grp: 8 (over z, y).
Axes of the slice: x: 2, y: 2, z: 4, core: 2. Of those that a mesh axis runs over, the one named last changes fastest.
Arguments:
- old_phi: float32 [4, 128, 32, 1024], P('box', 'grp'), may hold values from -6 to 6
- old_rhs: float32 [4, 128, 32, 1024], P('box', 'grp'), may hold values from -12 to 12
- old_beta: float32 [4, 128, 32, 1024], P('box', 'grp'), may hold values from 0.25 to 4
- coarse_field: float32 [4, 128, 16, 256], P('box', 'grp'), may hold values from -6 to 6
- old_pos: int32 [128], P('grp'), may hold values from 0 to 127, each once
- refined: int32 [128], P('grp'), may hold values 0 or 1
- new_owner: int32 [128, 1], P('grp'), may hold values from 0 to 7; in each aligned block of 16 rows (0 to 15, 16 to 31, ...) at most 2 rows name the same one
Outputs:
- smoothed: float32 [4, 128, 32, 1024], P('box', 'grp')
Inputs may be any that keep to these rules, and one draw needn't show every extreme that they name: `old_pos`: a permutation of the positions of one slab. `new_owner`: in each device's aligned block of 16 slots no owner is named more than 2 times, a bound that some block reaches.
All inputs are finite; a program needn't handle non-finite values. No bound on the sum of `refined` on one device may be relied on, other than what follows from the above.
Results may differ from a plain program's by a relative error of at most 0.000082.
Values sent between devices are 32-bit elements; how exact they have to be, the bound alone decides.
A program may use at most 256 MiB of HBM per device.

v0:
```python
import functools

import jax
import jax.numpy as jnp
import numpy as np
from jax import lax
from jax.experimental import pallas as pl
from jax.experimental.pallas import tpu as pltpu
from jax.sharding import PartitionSpec as P

CAP = 2
LANES = 128
PHI, BETA, COARSE, META, ROWS = 0, 32, 64, 80, 88
OUTSIDE = -(1 << 20)
STEPS = ((-1, 0), (1, 0), (0, -1), (0, 1))
HIGHEST = lax.Precision.HIGHEST


def turn(x, shift, axis=1):
    shift = shift % x.shape[axis]
    return x if shift == 0 else pltpu.roll(x, shift, axis)


def lane_of(shape):
    return lax.broadcasted_iota(jnp.int32, shape, 1)


def groups_of(x):
    return [x[:, LANES * g : LANES * (g + 1)] for g in range(x.shape[1] // LANES)]


def faces(parts):
    lane = lane_of(parts[0].shape)
    m, a = lane % 32, lane // 32
    tile = jnp.zeros_like(parts[0])
    for g, part in enumerate(parts):
        tile = jnp.where(m == g, turn(part, g), tile)
        tile = jnp.where(m == 16 + g, turn(part, g - 15), tile)
    for k in range(4):
        here = a == k
        tile = jnp.where(here & (m >= 8) & (m < 16), turn(parts[0], 24 * k + 8), tile)
        tile = jnp.where(here & (m >= 24), turn(parts[-1], 24 * k - 72), tile)
    return tile


def spread(tile):
    lane = lane_of(tile.shape)
    m = lane % 32
    along_z = [jnp.where(m == 31, turn(tile, 15 - g), turn(tile, -g)) for g in range(8)]
    low = turn(tile, -8)
    high = turn(tile, 72)
    for a in range(1, 4):
        low = jnp.where(lane // 8 == a, turn(tile, -24 * a - 8), low)
        high = jnp.where((lane - 96) // 8 == a, turn(tile, 72 - 24 * a), high)
    return along_z, low, high


def swapped(tiles):
    m = lane_of(tiles[0].shape) % 32
    pick = jnp.where(m < 8, tiles[3], jnp.where(m < 16, tiles[1], jnp.where(m < 24, tiles[2], tiles[0])))
    return jnp.where(m < 16, turn(pick, -16), turn(pick, 16))


def around(parts, ghost, low_x, high_x, g):
    along_z, low_y, high_y = ghost
    x = parts[g]
    lane = lane_of(x.shape)
    m = lane % 32
    row = lax.broadcasted_iota(jnp.int32, x.shape, 0)
    cut = slice(LANES * g, LANES * (g + 1))
    minus_x = jnp.where(row == 0, low_x[:, cut], turn(x, 1, 0))
    plus_x = jnp.where(row == x.shape[0] - 1, high_x[:, cut], turn(x, -1, 0))
    if g == 0:
        minus_y = jnp.where(lane < 32, low_y, turn(x, 32))
    else:
        minus_y = turn(jnp.where(lane >= 96, parts[g - 1], x), 32)
    if g == len(parts) - 1:
        plus_y = jnp.where(lane >= 96, high_y, turn(x, -32))
    else:
        plus_y = turn(jnp.where(lane < 32, parts[g + 1], x), -32)
    minus_z = jnp.where(m == 0, along_z[g], turn(x, 1))
    plus_z = jnp.where(m == 31, along_z[g], turn(x, -1))
    return [minus_x, plus_x, minus_y, plus_y, minus_z, plus_z]


def half_sweep(colour, phi, rhs, beta, phi_tile, beta_tile, phi_x, beta_x):
    phis, rhss, betas = groups_of(phi), groups_of(rhs), groups_of(beta)
    phi_ghost, beta_ghost = spread(phi_tile), spread(beta_tile)
    out = []
    for g in range(len(phis)):
        b = betas[g]
        near_b = around(betas, beta_ghost, beta_x[0], beta_x[1], g)
        near_p = around(phis, phi_ghost, phi_x[0], phi_x[1], g)
        lane = lane_of(b.shape)
        row = lax.broadcasted_iota(jnp.int32, b.shape, 0)
        accum, total = 0.5 * rhss[g] / b, jnp.zeros_like(b)
        for other, value in zip(near_b, near_p):
            other = jnp.where(other > 0.0, other, b)
            ratio = other / (b + other)
            accum = accum + ratio * value
            total = total + ratio
        mine = (row + lane // 32 + lane) % 2 == colour
        out.append(jnp.where(mine, accum / total, phis[g]))
    return out


def pack_kernel(count, pos, ref, own, phi, beta, coarse, pick, sent, up, down):
    half = coarse.shape[1]
    wide = jnp.dot(
        coarse[...].reshape(count * half, coarse.shape[2]), pick[...],
        precision=HIGHEST, preferred_element_type=jnp.float32,
    )
    lane = lane_of((8, LANES))
    for q in range(count):
        sent[q, COARSE:META, :] = wide[q * half : (q + 1) * half]
        meta = jnp.where(lane == 0, pos[q], jnp.where(lane == 1, ref[q], own[q]))
        sent[q, META:ROWS, :] = meta.astype(jnp.float32)

    def one(q, carry):
        sent[q, PHI:BETA, :] = faces(groups_of(phi[q]))
        sent[q, BETA:COARSE, :] = faces(groups_of(beta[q]))
        down[q, 0:1, :] = phi[q, 0:1, :]
        down[q, 1:2, :] = beta[q, 0:1, :]
        up[q, 0:1, :] = phi[q, 31:32, :]
        up[q, 1:2, :] = beta[q, 31:32, :]
        return carry

    lax.fori_loop(0, count, one, 0)


def first_kernel(
    count, slots, meta, pos, own, phi, rhs, beta, got, low, high,
    out, tile, up, down, beta_tile, coarse_tile, near, source, holder, filled, wide,
):
    q = pl.program_id(0)
    groups = slots // count

    @pl.when(q == 0)
    def _():
        def place(s, carry):
            holder[meta[s]] = s
            return carry

        lax.fori_loop(0, slots, place, 0)

        def clear(s, carry):
            source[s] = -1
            return carry

        lax.fori_loop(0, groups * CAP, clear, 0)

        def empty(s, carry):
            filled[s] = 0
            return carry

        lax.fori_loop(0, groups, empty, 0)

        def give(s, carry):
            to = own[s]
            rank = filled[to]
            filled[to] = rank + 1
            live = meta[slots + pos[s]] > 0
            source[to * CAP + rank] = jnp.where(live, s, -1)
            return carry

        lax.fori_loop(0, count, give, 0)

    here = pos[q]
    row, col = lax.div(here, count), lax.rem(here, count)
    fine_phi, fine_beta, under = [], [], []
    for k, (dy, dz) in enumerate(STEPS):
        y, z = row + dy, col + dz
        inside = (y >= 0) & (y < groups) & (z >= 0) & (z < count)
        spot = jnp.where(inside, y * count + z, 0)
        fine = inside & (meta[slots + spot] > 0)
        slot = holder[spot]
        near[q * 4 + k] = jnp.where(fine, slot, -1)
        fine_phi.append(jnp.where(fine, got[slot, PHI:BETA, :], 0.0))
        fine_beta.append(jnp.where(fine, got[slot, BETA:COARSE, :], 0.0))
        under.append(jnp.where(inside & jnp.logical_not(fine), got[spot, COARSE:META, :], 0.0))
    narrow = swapped(under)
    half = narrow.shape[0]
    wide[pl.ds(0, half, stride=2), :] = narrow
    wide[pl.ds(1, half, stride=2), :] = narrow
    coarse_ghost = wide[...]
    beta_ghost = swapped(fine_beta)
    coarse_tile[0] = coarse_ghost
    beta_tile[0] = beta_ghost
    parts = half_sweep(
        0, phi[0], rhs[0], beta[0], swapped(fine_phi) + coarse_ghost, beta_ghost,
        (low[0, 0:1, :], high[0, 0:1, :]), (low[0, 1:2, :], high[0, 1:2, :]),
    )
    for g, part in enumerate(parts):
        cut = slice(LANES * g, LANES * (g + 1))
        out[0, :, cut] = part
        down[0, :, cut] = part[0:1]
        up[0, :, cut] = part[31:32]
    tile[0] = faces(parts)


def second_kernel(
    near, source, phi, rhs, beta, got, low, high, low_b, high_b, beta_tile, coarse_tile, out
):
    q = source[pl.program_id(0)]

    @pl.when(q < 0)
    def _():
        out[...] = jnp.zeros_like(out)

    @pl.when(q >= 0)
    def _():
        fine_phi = []
        for k in range(4):
            slot = near[q * 4 + k]
            fine_phi.append(jnp.where(slot >= 0, got[jnp.maximum(slot, 0)], 0.0))
        parts = half_sweep(
            1, phi[0], rhs[0], beta[0], swapped(fine_phi) + coarse_tile[0], beta_tile[0],
            (low[0], high[0]), (low_b[0, 1:2, :], high_b[0, 1:2, :]),
        )
        for g, part in enumerate(parts):
            out[0, :, LANES * g : LANES * (g + 1)] = part


def coarse_pick(half):
    lane = np.arange(LANES)
    m, a = lane % 32, lane // 32
    j = m % 8
    y = np.select([m < 8, m < 16, m < 24], [4 * j + a, 0 * a, 4 * j + a], 2 * half - 1 + 0 * a)
    z = np.select([m < 8, m < 16, m < 24], [0 * a, 8 * a + j, 2 * half - 1 + 0 * a], 8 * a + j)
    cell = (y // 2) * half + z // 2
    return (np.arange(half * half)[:, None] == cell[None, :]).astype(np.float32)


def struct(*shape, dtype=jnp.float32):
    return jax.ShapeDtypeStruct(shape, dtype)


def gathered(x):
    return lax.all_gather(x, "grp", axis=0, tiled=True)


def slab_shift(up, down):
    size = lax.axis_size("box")
    ahead = [(i, i + 1) for i in range(size - 1)]
    back = [(j, i) for i, j in ahead]
    return lax.ppermute(up, "box", ahead), lax.ppermute(down, "box", back)


def shards(old_phi, old_rhs, old_beta, coarse_field, old_pos, refined, new_owner):
    phi, rhs, beta, coarse = old_phi[0], old_rhs[0], old_beta[0], coarse_field[0]
    count, edge, area = phi.shape
    groups = lax.axis_size("grp")
    slots = count * groups
    owner = new_owner[:, 0]
    vmem = pl.BlockSpec(memory_space=pltpu.VMEM)
    smem = pl.BlockSpec(memory_space=pltpu.SMEM)
    params = pltpu.CompilerParams(vmem_limit_bytes=48 * 1024 * 1024)
    sent, up, down = pl.pallas_call(
        functools.partial(pack_kernel, count),
        out_shape=(struct(count, ROWS, LANES), struct(count, 2, area), struct(count, 2, area)),
        in_specs=[smem, smem, smem, vmem, vmem, vmem, vmem],
        out_specs=(vmem, vmem, vmem),
        compiler_params=params,
        name="pack",
    )(old_pos, refined, owner, phi, beta, coarse, jnp.asarray(coarse_pick(edge // 2)))
    got = gathered(sent)
    low, high = slab_shift(up, down)
    meta = got[:, META, 0:3].astype(jnp.int32).T.reshape(3 * slots)

    def own(*shape):
        return pl.BlockSpec((1,) + shape, lambda q, *_: (q, 0, 0))

    def full(*shape):
        return pl.BlockSpec(shape, lambda q, *_: (0, 0, 0))

    box = own(edge, area)
    middle, tile, up2, down2, beta_tile, coarse_tile, near, source = pl.pallas_call(
        functools.partial(first_kernel, count, slots),
        out_shape=(
            struct(count, edge, area), struct(count, edge, LANES), struct(count, 1, area),
            struct(count, 1, area), struct(count, edge, LANES), struct(count, edge, LANES),
            struct(count * 4, dtype=jnp.int32), struct(groups * CAP, dtype=jnp.int32),
        ),
        grid_spec=pltpu.PrefetchScalarGridSpec(
            num_scalar_prefetch=3,
            grid=(count,),
            in_specs=[box, box, box, full(slots, ROWS, LANES), own(2, area), own(2, area)],
            out_specs=[
                box, own(edge, LANES), own(1, area), own(1, area), own(edge, LANES),
                own(edge, LANES), smem, smem,
            ],
            scratch_shapes=[
                pltpu.SMEM((slots,), jnp.int32), pltpu.SMEM((groups,), jnp.int32),
                pltpu.VMEM((edge, LANES), jnp.float32),
            ],
        ),
        compiler_params=params,
        name="colour0",
    )(meta, old_pos, owner, phi, rhs, beta, got, low, high)
    got2 = gathered(tile)
    low2, high2 = slab_shift(up2, down2)

    def at(*shape):
        return pl.BlockSpec(
            (1,) + shape, lambda r, near, source: (jnp.maximum(source[r], 0), 0, 0)
        )

    ordered = pl.pallas_call(
        second_kernel,
        out_shape=struct(groups * CAP, edge, area),
        grid_spec=pltpu.PrefetchScalarGridSpec(
            num_scalar_prefetch=2,
            grid=(groups * CAP,),
            in_specs=[
                at(edge, area), at(edge, area), at(edge, area), full(slots, edge, LANES),
                at(1, area), at(1, area), at(2, area), at(2, area), at(edge, LANES),
                at(edge, LANES),
            ],
            out_specs=[box][0],
        ),
        compiler_params=params,
        name="colour1",
    )(near, source, middle, rhs, beta, got2, low2, high2, low, high, beta_tile, coarse_tile)
    moved = lax.all_to_all(
        ordered.reshape(groups, CAP, edge, area), "grp", split_axis=0, concat_axis=0, tiled=True
    )
    return moved.reshape(groups * CAP, edge, area)[None]


def solution(mesh):
    return jax.shard_map(
        shards,
        mesh=mesh,
        in_specs=(
            P("box", "grp", None, None),
            P("box", "grp", None, None),
            P("box", "grp", None, None),
            P("box", "grp", None, None),
            P("grp"),
            P("grp"),
            P("grp", None),
        ),
        out_specs=P("box", "grp", None, None),
        check_vma=False,
    )
```

profile of v0, /device:TPU:0, one launch (start us, length us, event | category | flops | bytes accessed | tf_op | source)
XLA Modules:
  0.0 258.8 jit_solution(8865629267243389359)
XLA Ops:
  6.5 0.0 all-gather.3.cloned.1.call-start
  6.5 0.0 copy-start
  6.5 1.6 copy-done
  8.1 0.0 copy-start.1
  8.1 1.6 copy-done.1
  9.7 0.0 copy-start.5
  9.7 0.9 copy-done.5
  10.7 0.0 copy-start.6
  10.7 0.9 copy-done.6
  11.6 0.0 copy-start.7
  11.6 0.7 copy-done.7
  12.2 0.0 copy-start.9
  12.2 0.7 copy-done.9
  12.9 0.0 copy-start.11
  12.9 0.7 copy-done.11
  13.5 0.0 copy-start.2
  13.5 0.0 copy-start.8
  13.5 0.0 copy-start.10
  13.5 5.9 %pack.1 = (f32[16,88,128]{2,1,0:T(8,128)}, f32[16,2,1024]{2,1,0:T(2,128)S(1)}, f32[16,2,1024]{2,1,0:T(2,128)S(1)}) custom-call(s32[16]{0:T(128)S(1)} %copy-done.7, s32[16]{0:T(128)S(1)} %copy-done.11, s32[16]{0:T(128)S(1)} %bitcast.19, f32[16,32,1024]{2,1,0:T(8,128)S(1)} %bitcast.15, f32[16,32,1024]{2,1,0:T(8,128)S(1)} %bitcast.13, ...), custom_call_target="tpu_custom_call" | custom-call | tf_op jit(solution)/shard_map/pack/pallas_call | solution.py:258
  19.4 0.0 all-gather.3.cloned.1.call-update
  19.4 0.0 all-gather.5.cloned.1.call-start
  19.5 2.4 collective-permute-start
  21.9 1.3 collective-permute-start.1
  23.2 91.8 %all-gather.3.cloned.1.call-done.got = f32[128,88,128]{2,1,0:T(8,128)} async-done(((f32[16,88,128]{2,1,0:T(8,128)}), f32[128,88,128]{2,1,0:T(8,128)}) %all-gather.3.cloned.1.call-update) | async-done | bytes 5767184 | tf_op jit(solution)/shard_map/all_gather | solution.py:239
  114.9 1.1 slice_convert_fusion
  116.0 0.1 copy.10
  116.1 0.0 collective-permute-done.low.low_b
  116.1 0.0 collective-permute-done.1.high.high_b
  116.1 0.0 copy-done.2
  116.1 0.0 copy-done.8
  116.1 0.0 copy-done.10
  116.1 17.9 %colour0.1 = (f32[16,32,1024]{2,1,0:T(8,128)S(1)}, f32[16,32,128]{2,1,0:T(8,128)}, f32[16,1,1024]{2,1,0:T(1,128)S(1)}, f32[16,1,1024]{2,1,0:T(1,128)S(1)}, f32[1...) custom-call(s32[384]{0:T(512)S(1)} %bitcast.18, s32[16]{0:T(128)S(1)} %copy-done.8, ...), custom_call_target="tpu_custom_call" | custom-call | tf_op jit(solution)/shard_map/colour0/pallas_call | solution.py:277
  134.1 0.0 copy-start.3
  134.1 1.3 copy-done.3
  135.4 0.0 all-gather.5.cloned.1.call-update
  135.4 1.3 collective-permute-start.2
  136.7 1.3 collective-permute-start.3
  138.0 0.0 collective-permute-done.2.low
  138.0 3.5 %collective-permute-done.3.high = f32[16,1,1024]{2,1,0:T(1,128)S(1)} collective-permute-done((f32[16,1,1024]{2,1,0:T(1,128)S(1)}, f32[16,1,1024]{2,1,0:T(1,128)S(1)}, u32[]{:S(2)}, u32[]{:S(2)}) %collective-permute-start.3) | collective-permute-done | bytes 65568 | tf_op jit(solution)/shard_map/ppermute | solution.py:246
  141.6 41.5 %all-gather.5.cloned.1.call-done.got = f32[128,32,128]{2,1,0:T(8,128)} async-done(((f32[16,32,128]{2,1,0:T(8,128)}), f32[128,32,128]{2,1,0:T(8,128)}) %all-gather.5.cloned.1.call-update) | async-done | bytes 2097168 | tf_op jit(solution)/shard_map/all_gather | solution.py:239
  183.1 0.0 copy-start.4
  183.1 1.6 copy-done.4
  184.6 13.7 %colour1.1 = f32[16,32,1024]{2,1,0:T(8,128)S(1)} custom-call(s32[64]{0:T(128)S(1)} %get-tuple-element.19.near, s32[16]{0:T(128)S(1)} %get-tuple-element.20.source, f32[16,32,1024]{2,1,0:T(8,128)S(1)} %copy-done.4, f32[16,32,1024]{2,1,0:T(8,128)} %bitcast.23, f32[16,32,1024]{2,1,0:T(8,128)} %bitcast.12, f32[128,32,128]{2,1,0:T(8,128)} %all-gather.5.cloned.1.call-done.got, ...), custom_call_target="tpu_custom_call" | custom-call | tf_op jit(solution)/shard_map/colour1/pallas_call | solution.py:308
  198.4 52.3 %all_to_all.5 = f32[8,2,32,1024]{3,2,1,0:T(8,128)S(1)} all-to-all(f32[8,2,32,1024]{3,2,1,0:T(8,128)S(1)} %bitcast.14), channel_id=1, replica_groups=mesh['box'=4,'grp'=8] {'grp'}, dimensions={0} | all-to-all | bytes 4194304 | tf_op jit(solution)/shard_map/all_to_all | solution.py:324
  250.7 1.3 copy.12
Async XLA Ops:
  6.5 108.4 %all-gather.3.cloned.1.call-start = ((), (), s32[]{:S(2)}) async-start(), calls=%async_computation.1 | async-start | bytes 6488064 | tf_op jit(solution)/shard_map/all_gather | solution.py:239
  6.5 1.6 copy-start
  8.1 1.6 copy-start.1
  9.7 0.9 copy-start.5
  10.7 0.9 copy-start.6
  11.6 0.7 copy-start.7
  12.2 0.7 copy-start.9
  12.9 0.7 copy-start.11
  13.5 102.6 %copy-start.2 = (f32[1,16,32,1024]{3,2,1,0:T(8,128)S(1)}, f32[1,16,32,1024]{3,2,1,0:T(8,128)}, u32[]{:S(2)}) copy-start(f32[1,16,32,1024]{3,2,1,0:T(8,128)} %param.8) | copy-start | bytes 6291460
  13.5 102.6 %copy-start.8 = (s32[16]{0:T(128)S(1)}, s32[16]{0:T(128)}, u32[]{:S(2)}) copy-start(s32[16]{0:T(128)} %pos.3) | copy-start | bytes 196
  13.5 102.6 %copy-start.10 = (s32[16,1]{0,1:T(1,128)S(1)}, s32[16,1]{0,1:T(1,128)}, u32[]{:S(2)}) copy-start(s32[16,1]{0,1:T(1,128)} %param.14) | copy-start | bytes 196
  19.4 163.6 %all-gather.5.cloned.1.call-start = ((), (), s32[]{:S(2)}) async-start(), calls=%async_computation.2 | async-start | bytes 2359296 | tf_op jit(solution)/shard_map/all_gather | solution.py:239
  19.5 96.6 %collective-permute-start = (f32[16,2,1024]{2,1,0:T(2,128)S(1)}, f32[16,2,1024]{2,1,0:T(2,128)S(1)}, u32[]{:S(2)}, u32[]{:S(2)}) collective-permute-start(f32[16,2,1024]{2,1,0:T(2,128)S(1)} %get-tuple-element.17), channel_id=1, source_target_pairs={{0,8},{8,16},{16,24},{1,9},{9,17},{17,25},{2,10},{10,18},{18,26},{... | collective-permute-start | bytes 393224 | tf_op jit(solution)/shard_map/ppermute | solution.py:246
  21.9 94.2 %collective-permute-start.1 = (f32[16,2,1024]{2,1,0:T(2,128)S(1)}, f32[16,2,1024]{2,1,0:T(2,128)S(1)}, u32[]{:S(2)}, u32[]{:S(2)}) collective-permute-start(f32[16,2,1024]{2,1,0:T(2,128)S(1)} %get-tuple-element.18), channel_id=1, source_target_pairs={{8,0},{16,8},{24,16},{9,1},{17,9},{25,17},{10,2},{18,10},{26,18},{... | collective-permute-start | bytes 393224 | tf_op jit(solution)/shard_map/ppermute | solution.py:246
  134.1 1.3 copy-start.3
  135.4 2.6 %collective-permute-start.2 = (f32[16,1,1024]{2,1,0:T(1,128)S(1)}, f32[16,1,1024]{2,1,0:T(1,128)S(1)}, u32[]{:S(2)}, u32[]{:S(2)}) collective-permute-start(f32[16,1,1024]{2,1,0:T(1,128)S(1)} %get-tuple-element.23), channel_id=1, source_target_pairs={{0,8},{8,16},{16,24},{1,9},{9,17},{17,25},{2,10},{10,18},{18,26},{... | collective-permute-start | bytes 196616 | tf_op jit(solution)/shard_map/ppermute | solution.py:246
  136.7 4.8 %collective-permute-start.3 = (f32[16,1,1024]{2,1,0:T(1,128)S(1)}, f32[16,1,1024]{2,1,0:T(1,128)S(1)}, u32[]{:S(2)}, u32[]{:S(2)}) collective-permute-start(f32[16,1,1024]{2,1,0:T(1,128)S(1)} %get-tuple-element.24), channel_id=1, source_target_pairs={{8,0},{16,8},{24,16},{9,1},{17,9},{25,17},{10,2},{18,10},{26,18},{... | collective-permute-start | bytes 196616 | tf_op jit(solution)/shard_map/ppermute | solution.py:246
  183.1 1.6 copy-start.4
Sparse Core Ops, SparseCore 0:
  19.6 95.3 all-gather.2
  135.5 47.4 all-gather.4
where the time goes:
time: 260 us; the launch traced here: 259 us
  waiting for transfers between devices  137 us (53%)
  blocking collectives  52.3 us (20%)
  Pallas kernels  37.5 us (14%)
  between operations  13.5 us (5%)
  local copies, waits for them, and re-layouts  11.3 us (4%)
  starting transfers between devices  6.28 us (2%)
    all_gather x2, waiting for transfers between devices, gathered(): return lax.all_gather(x, 'grp', axis=0, tiled=True)  133 us
    all_to_all x1, blocking collectives, shards(): lax.all_to_all(ordered.reshape(groups, CAP, edge, area), 'grp', split_axi...  52.3 us
    pallas_call x1, Pallas kernels, shards(): pl.pallas_call(functools.partial(first_kernel, count, slots), out_shape=(...  17.9 us
    pallas_call x1, Pallas kernels, shards(): pl.pallas_call(second_kernel, out_shape=struct(groups * CAP, edge, area),...  13.7 us
    unnamed x25, local copies, waits for them, and re-layouts  11.2 us
    ppermute x4, starting transfers between devices, slab_shift(): return (lax.ppermute(up, 'box', ahead), lax.ppermute(down, 'box', back))  6.24 us
    pallas_call x1, Pallas kernels, shards(): pl.pallas_call(functools.partial(pack_kernel, count), out_shape=(struct(c...  5.87 us
  transfers between devices with their start and end apart: 6, of which 3 were waited for; matrix products, arithmetic and copies ran while one was open for 0% of the time, Pallas kernels for 0%

commit v1 on v0

--- a/solution.py
+++ b/solution.py
@@ -10,8 +10,9 @@
 
 CAP = 2
 LANES = 128
-PHI, BETA, COARSE, META, ROWS = 0, 32, 64, 80, 88
-OUTSIDE = -(1 << 20)
+FACES, COARSE = 32, 8
+ROWS = FACES + COARSE
+OUTER = 4
 STEPS = ((-1, 0), (1, 0), (0, -1), (0, 1))
 HIGHEST = lax.Precision.HIGHEST
 
@@ -104,41 +105,186 @@
     return out
 
 
-def pack_kernel(count, pos, ref, own, phi, beta, coarse, pick, sent, up, down):
+def face_colour(shape):
+    lane = lane_of(shape)
+    m, a = lane % 32, lane // 32
+    row = lax.broadcasted_iota(jnp.int32, shape, 0)
+    return (row + jnp.where((m & 8) == 0, a, m) + m // 16) % 2
+
+
+def paired(x, axis):
+    even = lax.broadcasted_iota(jnp.int32, x.shape, axis) % 2 == 0
+    return jnp.where(even, turn(x, -1, axis), turn(x, 1, axis))
+
+
+def mixed(colour, phi, beta):
+    return jnp.where(face_colour(phi.shape) == colour, phi, paired(beta, 0))
+
+
+def mixed_row(colour, first, phi, beta):
+    lane = lane_of(phi.shape)
+    return jnp.where((first + lane // 32 + lane) % 2 == colour, phi, paired(beta, 1))
+
+
+def folded(x):
+    lane = lane_of((COARSE, LANES))
+    odd = jnp.where((lane & 8) == 0, lane // 32, lane) % 2 == 1
+    return jnp.where(odd, x[COARSE:], x[:COARSE])
+
+
+def unfolded(t):
+    lane = lane_of(t.shape)
+    along_z = (lane & 8) == 0
+    odd = jnp.where(along_z, lane // 32, lane) % 2 == 1
+    low = jnp.where(odd, jnp.where(along_z, turn(t, 32), turn(t, 1)), t)
+    high = jnp.where(odd, t, jnp.where(along_z, turn(t, -32), turn(t, -1)))
+    return low, high
+
+
+def pack_kernel(count, pos, ref, phi, beta, coarse, pick, sent, up, down):
     half = coarse.shape[1]
     wide = jnp.dot(
         coarse[...].reshape(count * half, coarse.shape[2]), pick[...],
         precision=HIGHEST, preferred_element_type=jnp.float32,
     )
     lane = lane_of((8, LANES))
+    row = lax.broadcasted_iota(jnp.int32, (8, LANES), 0)
+    meta = jnp.zeros((8, LANES), jnp.int32)
     for q in range(count):
-        sent[q, COARSE:META, :] = wide[q * half : (q + 1) * half]
-        meta = jnp.where(lane == 0, pos[q], jnp.where(lane == 1, ref[q], own[q]))
-        sent[q, META:ROWS, :] = meta.astype(jnp.float32)
+        sent[q * ROWS + FACES : (q + 1) * ROWS, :] = folded(wide[q * half : (q + 1) * half])
+        meta = jnp.where((lane == q) & (row == 0), pos[q], meta)
+        meta = jnp.where((lane == q) & (row == 1), ref[q], meta)
+    sent[count * ROWS :, :] = meta.astype(jnp.float32)
 
     def one(q, carry):
-        sent[q, PHI:BETA, :] = faces(groups_of(phi[q]))
-        sent[q, BETA:COARSE, :] = faces(groups_of(beta[q]))
-        down[q, 0:1, :] = phi[q, 0:1, :]
-        down[q, 1:2, :] = beta[q, 0:1, :]
-        up[q, 0:1, :] = phi[q, 31:32, :]
-        up[q, 1:2, :] = beta[q, 31:32, :]
+        tile = mixed(1, faces(groups_of(phi[q])), faces(groups_of(beta[q])))
+        sent[pl.ds(pl.multiple_of(q * ROWS, 8), FACES), :] = tile
+        down[q] = mixed_row(1, 0, phi[q, 0:1, :], beta[q, 0:1, :])
+        up[q] = mixed_row(1, 1, phi[q, 31:32, :], beta[q, 31:32, :])
         return carry
 
     lax.fori_loop(0, count, one, 0)
+
+
+def exchange_kernel(n, slabs, sent, up, down, got, low, high, send, recv, x_send, x_recv, local):
+    inner = n // OUTER
+    me, slab = lax.axis_index("grp"), lax.axis_index("box")
+    z, y = me // inner, me % inner
+
+    def device(to):
+        return {"grp": to}
+
+    ends = [(z < OUTER - 1, "grp", me + inner), (z > 0, "grp", me - inner),
+            (slab < slabs - 1, "box", slab + 1), (slab > 0, "box", slab - 1)]
+    mates = [z * inner + (y + i) % inner for i in range(1, inner)]
+    barrier = pltpu.get_barrier_semaphore()
+    for there, axis, to in ends:
+        @pl.when(there)
+        def _(axis=axis, to=to):
+            pl.semaphore_signal(barrier, inc=1, device_id={axis: to}, device_id_type=pl.DeviceIdType.MESH)
+    for to in mates:
+        pl.semaphore_signal(barrier, inc=1, device_id=device(to), device_id_type=pl.DeviceIdType.MESH)
+    total = inner - 1
+    for there, _, _ in ends:
+        total = total + there.astype(jnp.int32)
+    pl.semaphore_wait(barrier, total)
+
+    def copy(src, block, lane, to):
+        return pltpu.make_async_remote_copy(
+            src_ref=src, dst_ref=got.at[block], send_sem=send.at[lane, block],
+            recv_sem=recv.at[block], device_id=device(to), device_id_type=pl.DeviceIdType.MESH,
+        )
+
+    def beside(block, src):
+        for i, to in enumerate(mates):
+            copy(src, block, 2 + i, to).start()
+
+    def along_x(src, dst, lane, to):
+        return pltpu.make_async_remote_copy(
+            src_ref=src, dst_ref=dst, send_sem=x_send.at[lane], recv_sem=x_recv.at[lane],
+            device_id={"box": to}, device_id_type=pl.DeviceIdType.MESH,
+        )
+
+    pl.when(z < OUTER - 1)(lambda: copy(sent, me, 0, me + inner).start())
+    pl.when(z > 0)(lambda: copy(sent, me, 1, me - inner).start())
+    beside(me, sent)
+    pl.when(slab < slabs - 1)(lambda: along_x(up, low, 0, slab + 1).start())
+    pl.when(slab > 0)(lambda: along_x(down, high, 1, slab - 1).start())
+    own = pltpu.make_async_copy(sent, got.at[me], local)
+    own.start()
+    for s in range(1, OUTER):
+        @pl.when(z >= s)
+        def _(s=s):
+            block = me - s * inner
+            copy(got.at[block], block, 0, block).wait_recv()
+            pl.when(z < OUTER - 1)(lambda: copy(got.at[block], block, 0, me + inner).start())
+            beside(block, got.at[block])
+
+        @pl.when(z + s < OUTER)
+        def _(s=s):
+            block = me + s * inner
+            copy(got.at[block], block, 1, block).wait_recv()
+            pl.when(z > 0)(lambda: copy(got.at[block], block, 1, me - inner).start())
+            beside(block, got.at[block])
+    for level in range(OUTER):
+        for i, to in enumerate(mates):
+            block = level * inner + (y + i + 1) % inner
+            copy(got.at[block], block, 2, to).wait_recv()
+    own.wait()
+    pl.when(slab > 0)(lambda: along_x(up, low, 0, slab - 1).wait_recv())
+    pl.when(slab < slabs - 1)(lambda: along_x(down, high, 1, slab + 1).wait_recv())
+    for level in range(OUTER):
+        block = level * inner + y
+        pl.when((z < OUTER - 1) & (level <= z))(lambda: copy(sent, block, 0, me + inner).wait_send())
+        pl.when((z > 0) & (level >= z))(lambda: copy(sent, block, 1, me - inner).wait_send())
+        for i, to in enumerate(mates):
+            copy(sent, block, 2 + i, to).wait_send()
+    pl.when(slab < slabs - 1)(lambda: along_x(up, low, 0, slab + 1).wait_send())
+    pl.when(slab > 0)(lambda: along_x(down, high, 1, slab - 1).wait_send())
+
+
+def exchanged(number, sent, up, down):
+    n, slabs = lax.axis_size("grp"), lax.axis_size("box")
+    anywhere = pl.BlockSpec(memory_space=pl.ANY)
+    return pl.pallas_call(
+        functools.partial(exchange_kernel, n, slabs),
+        out_shape=(struct(n, *sent.shape), struct(*up.shape), struct(*down.shape)),
+        in_specs=[anywhere] * 3,
+        out_specs=(anywhere,) * 3,
+        scratch_shapes=[
+            pltpu.SemaphoreType.DMA((1 + n // OUTER, n)), pltpu.SemaphoreType.DMA((n,)),
+            pltpu.SemaphoreType.DMA((2,)), pltpu.SemaphoreType.DMA((2,)), pltpu.SemaphoreType.DMA,
+        ],
+        compiler_params=pltpu.CompilerParams(collective_id=number, has_side_effects=True),
+        name="exchange",
+    )(sent, up, down)
+
+
+def halo_rows(low, high):
+    slab, slabs = lax.axis_index("box"), lax.axis_size("box")
+    below = jnp.where(slab > 0, low, 0.0)
+    above = jnp.where(slab < slabs - 1, high, 0.0)
+    return (below, above), (paired(below, 1), paired(above, 1))
 
 
 def first_kernel(
     count, slots, meta, pos, own, phi, rhs, beta, got, low, high,
-    out, tile, up, down, beta_tile, coarse_tile, near, source, holder, filled, wide,
+    out, tile, up, down, coarse_tile, near, source, holder, filled, wide,
 ):
     q = pl.program_id(0)
     groups = slots // count
 
+    def refined_at(p):
+        return meta[(lax.div(p, count) * 2 + 1) * count + lax.rem(p, count)] > 0
+
+    def rows(s, first, length):
+        start = pl.multiple_of(lax.rem(s, count) * ROWS + first, 8)
+        return got[lax.div(s, count), pl.ds(start, length), :]
+
     @pl.when(q == 0)
     def _():
         def place(s, carry):
-            holder[meta[s]] = s
+            holder[meta[lax.div(s, count) * 2 * count + lax.rem(s, count)]] = s
             return carry
 
         lax.fori_loop(0, slots, place, 0)
@@ -159,7 +305,7 @@
             to = own[s]
             rank = filled[to]
             filled[to] = rank + 1
-            live = meta[slots + pos[s]] > 0
+            live = refined_at(pos[s])
             source[to * CAP + rank] = jnp.where(live, s, -1)
             return carry
 
@@ -167,39 +313,36 @@
 
     here = pos[q]
     row, col = lax.div(here, count), lax.rem(here, count)
-    fine_phi, fine_beta, under = [], [], []
+    fine_tiles, under = [], []
     for k, (dy, dz) in enumerate(STEPS):
         y, z = row + dy, col + dz
         inside = (y >= 0) & (y < groups) & (z >= 0) & (z < count)
         spot = jnp.where(inside, y * count + z, 0)
-        fine = inside & (meta[slots + spot] > 0)
+        fine = inside & refined_at(spot)
         slot = holder[spot]
         near[q * 4 + k] = jnp.where(fine, slot, -1)
-        fine_phi.append(jnp.where(fine, got[slot, PHI:BETA, :], 0.0))
-        fine_beta.append(jnp.where(fine, got[slot, BETA:COARSE, :], 0.0))
-        under.append(jnp.where(inside & jnp.logical_not(fine), got[spot, COARSE:META, :], 0.0))
-    narrow = swapped(under)
-    half = narrow.shape[0]
-    wide[pl.ds(0, half, stride=2), :] = narrow
-    wide[pl.ds(1, half, stride=2), :] = narrow
+        fine_tiles.append(jnp.where(fine, rows(slot, 0, FACES), 0.0))
+        under.append(jnp.where(inside & jnp.logical_not(fine), rows(spot, FACES, COARSE), 0.0))
+    for i, narrow in enumerate(unfolded(swapped(under))):
+        for odd in range(2):
+            wide[pl.ds(2 * COARSE * i + odd, COARSE, stride=2), :] = narrow
     coarse_ghost = wide[...]
-    beta_ghost = swapped(fine_beta)
     coarse_tile[0] = coarse_ghost
-    beta_tile[0] = beta_ghost
+    ghost = swapped(fine_tiles)
+    phi_x, beta_x = halo_rows(low[0], high[0])
     parts = half_sweep(
-        0, phi[0], rhs[0], beta[0], swapped(fine_phi) + coarse_ghost, beta_ghost,
-        (low[0, 0:1, :], high[0, 0:1, :]), (low[0, 1:2, :], high[0, 1:2, :]),
+        0, phi[0], rhs[0], beta[0], ghost + coarse_ghost, paired(ghost, 0), phi_x, beta_x
     )
     for g, part in enumerate(parts):
         cut = slice(LANES * g, LANES * (g + 1))
         out[0, :, cut] = part
-        down[0, :, cut] = part[0:1]
-        up[0, :, cut] = part[31:32]
-    tile[0] = faces(parts)
+        down[0, :, cut] = mixed_row(0, 0, part[0:1], beta[0, 0:1, cut])
+        up[0, :, cut] = mixed_row(0, 1, part[31:32], beta[0, 31:32, cut])
+    tile[...] = mixed(0, faces(parts), faces(groups_of(beta[0])))
 
 
 def second_kernel(
-    near, source, phi, rhs, beta, got, low, high, low_b, high_b, beta_tile, coarse_tile, out
+    near, source, phi, rhs, beta, got, low, high, coarse_tile, out
 ):
     q = source[pl.program_id(0)]
 
@@ -209,13 +352,14 @@
 
     @pl.when(q >= 0)
     def _():
-        fine_phi = []
+        tiles = []
         for k in range(4):
             slot = near[q * 4 + k]
-            fine_phi.append(jnp.where(slot >= 0, got[jnp.maximum(slot, 0)], 0.0))
+            tiles.append(jnp.where(slot >= 0, got[jnp.maximum(slot, 0)], 0.0))
+        ghost = swapped(tiles)
+        phi_x, beta_x = halo_rows(low[0], high[0])
         parts = half_sweep(
-            1, phi[0], rhs[0], beta[0], swapped(fine_phi) + coarse_tile[0], beta_tile[0],
-            (low[0], high[0]), (low_b[0, 1:2, :], high_b[0, 1:2, :]),
+            1, phi[0], rhs[0], beta[0], ghost + coarse_tile[0], paired(ghost, 0), phi_x, beta_x
         )
         for g, part in enumerate(parts):
             out[0, :, LANES * g : LANES * (g + 1)] = part
@@ -233,17 +377,6 @@
 
 def struct(*shape, dtype=jnp.float32):
     return jax.ShapeDtypeStruct(shape, dtype)
-
-
-def gathered(x):
-    return lax.all_gather(x, "grp", axis=0, tiled=True)
-
-
-def slab_shift(up, down):
-    size = lax.axis_size("box")
-    ahead = [(i, i + 1) for i in range(size - 1)]
-    back = [(j, i) for i, j in ahead]
-    return lax.ppermute(up, "box", ahead), lax.ppermute(down, "box", back)
 
 
 def shards(old_phi, old_rhs, old_beta, coarse_field, old_pos, refined, new_owner):
@@ -257,15 +390,14 @@
     params = pltpu.CompilerParams(vmem_limit_bytes=48 * 1024 * 1024)
     sent, up, down = pl.pallas_call(
         functools.partial(pack_kernel, count),
-        out_shape=(struct(count, ROWS, LANES), struct(count, 2, area), struct(count, 2, area)),
-        in_specs=[smem, smem, smem, vmem, vmem, vmem, vmem],
+        out_shape=(struct(count * ROWS + 8, LANES), struct(count, 1, area), struct(count, 1, area)),
+        in_specs=[smem, smem, vmem, vmem, vmem, vmem],
         out_specs=(vmem, vmem, vmem),
         compiler_params=params,
         name="pack",
-    )(old_pos, refined, owner, phi, beta, coarse, jnp.asarray(coarse_pick(edge // 2)))
-    got = gathered(sent)
-    low, high = slab_shift(up, down)
-    meta = got[:, META, 0:3].astype(jnp.int32).T.reshape(3 * slots)
+    )(old_pos, refined, phi, beta, coarse, jnp.asarray(coarse_pick(edge // 2)))
+    got, low, high = exchanged(0, sent, up, down)
+    meta = got[:, count * ROWS : count * ROWS + 2, :count].astype(jnp.int32).reshape(2 * slots)
 
     def own(*shape):
         return pl.BlockSpec((1,) + shape, lambda q, *_: (q, 0, 0))
@@ -274,19 +406,19 @@
         return pl.BlockSpec(shape, lambda q, *_: (0, 0, 0))
 
     box = own(edge, area)
-    middle, tile, up2, down2, beta_tile, coarse_tile, near, source = pl.pallas_call(
+    middle, tile, up2, down2, coarse_tile, near, source = pl.pallas_call(
         functools.partial(first_kernel, count, slots),
         out_shape=(
-            struct(count, edge, area), struct(count, edge, LANES), struct(count, 1, area),
-            struct(count, 1, area), struct(count, edge, LANES), struct(count, edge, LANES),
+            struct(count, edge, area), struct(count * edge, LANES), struct(count, 1, area),
+            struct(count, 1, area), struct(count, edge, LANES),
             struct(count * 4, dtype=jnp.int32), struct(groups * CAP, dtype=jnp.int32),
         ),
         grid_spec=pltpu.PrefetchScalarGridSpec(
             num_scalar_prefetch=3,
             grid=(count,),
-            in_specs=[box, box, box, full(slots, ROWS, LANES), own(2, area), own(2, area)],
+            in_specs=[box, box, box, full(groups, count * ROWS + 8, LANES), own(1, area), own(1, area)],
             out_specs=[
-                box, own(edge, LANES), own(1, area), own(1, area), own(edge, LANES),
+                box, pl.BlockSpec((edge, LANES), lambda q, *_: (q, 0)), own(1, area), own(1, area),
                 own(edge, LANES), smem, smem,
             ],
             scratch_shapes=[
@@ -297,8 +429,7 @@
         compiler_params=params,
         name="colour0",
     )(meta, old_pos, owner, phi, rhs, beta, got, low, high)
-    got2 = gathered(tile)
-    low2, high2 = slab_shift(up2, down2)
+    got2, low2, high2 = exchanged(1, tile, up2, down2)
 
     def at(*shape):
         return pl.BlockSpec(
@@ -313,14 +444,13 @@
             grid=(groups * CAP,),
             in_specs=[
                 at(edge, area), at(edge, area), at(edge, area), full(slots, edge, LANES),
-                at(1, area), at(1, area), at(2, area), at(2, area), at(edge, LANES),
-                at(edge, LANES),
+                at(1, area), at(1, area), at(edge, LANES),
             ],
-            out_specs=[box][0],
+            out_specs=box,
         ),
         compiler_params=params,
         name="colour1",
-    )(near, source, middle, rhs, beta, got2, low2, high2, low, high, beta_tile, coarse_tile)
+    )(near, source, middle, rhs, beta, got2.reshape(slots, edge, LANES), low2, high2, coarse_tile)
     moved = lax.all_to_all(
         ordered.reshape(groups, CAP, edge, area), "grp", split_axis=0, concat_axis=0, tiled=True
     )

time: 260 us -> 180 us (0.69)
  waiting for transfers between devices: 137 us -> 0 us
  Pallas kernels: 37.5 us -> 108 us
  between operations: 13.5 us -> 0.1 us
  local copies, waits for them, and re-layouts: 11.3 us -> 17.9 us
  starting transfers between devices: 6.28 us -> 0 us
    all_gather x2 -> x0, waiting for transfers between devices: 133 us -> none  [gathered(): return lax.all_gather(x, 'grp', axis=0, tiled=True)]
    pallas_call x0 -> x2, Pallas kernels: none -> 68.5 us  [exchanged(): pl.pallas_call(functools.partial(exchange_kernel, n, slabs), out_shape=(s...]
    unnamed x25 -> x43, local copies, waits for them, and re-layouts: 11.2 us -> 17.8 us
    ppermute x4 -> x0, starting transfers between devices: 6.24 us -> none  [slab_shift(): return (lax.ppermute(up, 'box', ahead), lax.ppermute(down, 'box', back))]
    ppermute x4 -> x0, waiting for transfers between devices: 3.55 us -> none  [slab_shift(): return (lax.ppermute(up, 'box', ahead), lax.ppermute(down, 'box', back))]
  transfers between devices with their start and end apart: 6 -> 0, of which waited for: 3 -> 0; matrix products, arithmetic and copies ran while one was open for 0% -> 0% of each run, Pallas kernels for 0% -> 0%
where the time goes in v1:
time: 180 us; the launch traced here: 179 us
  Pallas kernels  108 us (60%)
  blocking collectives  52.4 us (29%)
  local copies, waits for them, and re-layouts  17.9 us (10%)
    pallas_call x2, Pallas kernels, exchanged(): pl.pallas_call(functools.partial(exchange_kernel, n, slabs), out_shape=(s...  68.5 us
    all_to_all x1, blocking collectives, shards(): lax.all_to_all(ordered.reshape(groups, CAP, edge, area), 'grp', split_axi...  52.4 us
    pallas_call x1, Pallas kernels, shards(): pl.pallas_call(functools.partial(first_kernel, count, slots), out_shape=(...  19.3 us
    unnamed x43, local copies, waits for them, and re-layouts  17.8 us
    pallas_call x1, Pallas kernels, shards(): pl.pallas_call(second_kernel, out_shape=struct(groups * CAP, edge, area),...  14.3 us
    pallas_call x1, Pallas kernels, shards(): pl.pallas_call(functools.partial(pack_kernel, count), out_shape=(struct(c...  5.66 us

profile of v1, /device:TPU:0, one launch (start us, length us, event | category | flops | bytes accessed | tf_op | source)
XLA Modules:
  0.0 178.9 jit_solution(3828303630912354709)
XLA Ops:
  0.0 0.0 copy-start
  0.0 1.6 copy-done
  1.6 0.0 copy-start.1
  1.6 1.6 copy-done.1
  3.2 0.0 copy-start.6
  3.2 0.9 copy-done.6
  4.1 0.0 copy-start.8
  4.1 0.9 copy-done.8
  5.0 0.0 copy-start.17
  5.0 0.7 copy-done.17
  5.7 0.7 copy-done.19
  6.4 0.0 copy-start.2
  6.4 0.0 copy-start.18
  6.4 5.7 %pack.1 = (f32[648,128]{1,0:T(8,128)S(1)}, f32[16,1,1024]{2,1,0:T(1,128)S(1)}, f32[16,1,1024]{2,1,0:T(1,128)S(1)}) custom-call(s32[16]{0:T(128)S(1)} %copy-done.17, s32[16]{0:T(128)S(1)} %copy-done.19, f32[16,32,1024]{2,1,0:T(8,128)S(1)} %bitcast.11, f32[16,32,1024]{2,1,0:T(8,128)S(1)} %bitcast.10, f32[16,16,256]{2,1,0:T(8,128)S(1)} %bitcast.14, ...), custom_call_target="tpu_custom_call" | custom-call | tf_op jit(solution)/shard_map/pack/pallas_call | solution.py:391
  12.0 0.0 copy-start.5
  12.0 0.7 copy-done.5
  12.8 0.0 copy-start.13
  12.8 0.6 copy-done.13
  13.4 0.0 copy-start.14
  13.4 0.6 copy-done.14
  14.0 40.8 %exchange.2 = (f32[8,648,128]{2,1,0:T(8,128)}, f32[16,1,1024]{2,1,0:T(1,128)}, f32[16,1,1024]{2,1,0:T(1,128)}) custom-call(f32[648,128]{1,0:T(8,128)} %copy-done.5, f32[16,1,1024]{2,1,0:T(1,128)} %copy-done.13, f32[16,1,1024]{2,1,0:T(1,128)} %copy-done.14), custom_call_target="tpu_custom_call" | custom-call | tf_op jit(solution)/shard_map/exchange/pallas_call | solution.py:249
  54.8 0.8 slice_convert_fusion
  55.6 0.1 reshape.9.meta
  55.7 0.0 copy-done.2
  55.7 0.0 copy-done.18
  55.7 0.0 copy-done.20
  55.7 0.0 copy-start.9
  55.7 0.8 copy-done.9
  56.6 0.0 copy-start.10
  56.6 0.8 copy-done.10
  57.4 19.3 %colour0.1 = (f32[16,32,1024]{2,1,0:T(8,128)S(1)}, f32[512,128]{1,0:T(8,128)S(1)}, f32[16,1,1024]{2,1,0:T(1,128)S(1)}, f32[16,1,1024]{2,1,0:T(1,128)S(1)}, f32[1...) custom-call(s32[256]{0:T(256)S(1)} %reshape.9.meta, s32[16]{0:T(128)S(1)} %copy-done.18, s32[16]{0:T(128)S(1)} %bitcast.15, ...), custom_call_target="tpu_custom_call" | custom-call | tf_op jit(solution)/shard_map/colour0/pallas_call | solution.py:409
  76.7 0.0 copy-start.3
  76.7 1.3 copy-done.3
  78.0 0.0 copy-start.7
  78.0 0.7 copy-done.7
  78.7 0.0 copy-start.15
  78.7 0.6 copy-done.15
  79.3 0.0 copy-start.16
  79.3 0.6 copy-done.16
  79.9 27.7 %exchange.3 = (f32[8,512,128]{2,1,0:T(8,128)}, f32[16,1,1024]{2,1,0:T(1,128)}, f32[16,1,1024]{2,1,0:T(1,128)}) custom-call(f32[512,128]{1,0:T(8,128)} %copy-done.7, f32[16,1,1024]{2,1,0:T(1,128)} %copy-done.15, f32[16,1,1024]{2,1,0:T(1,128)} %copy-done.16), custom_call_target="tpu_custom_call" | custom-call | tf_op jit(solution)/shard_map/exchange/pallas_call | solution.py:249
  107.6 0.0 copy-start.4
  107.6 1.6 copy-done.4
  109.2 0.0 copy-start.11
  109.2 0.8 copy-done.11
  110.1 0.8 copy-done.12
  110.9 14.3 %colour1.1 = f32[16,32,1024]{2,1,0:T(8,128)S(1)} custom-call(s32[64]{0:T(128)S(1)} %get-tuple-element.27.near, s32[16]{0:T(128)S(1)} %get-tuple-element.28.source, f32[16,32,1024]{2,1,0:T(8,128)S(1)} %copy-done.4, f32[16,32,1024]{2,1,0:T(8,128)} %bitcast.17, f32[16,32,1024]{2,1,0:T(8,128)} %bitcast.9, f32[128,32,128]{2,1,0:T(8,128)} %bitcast.19, ...), custom_call_target="tpu_custom_call" | custom-call | tf_op jit(solution)/shard_map/colour1/pallas_call | solution.py:439
  125.2 52.4 %all_to_all.5 = f32[8,2,32,1024]{3,2,1,0:T(8,128)S(1)} all-to-all(f32[8,2,32,1024]{3,2,1,0:T(8,128)S(1)} %bitcast.13), channel_id=1, replica_groups=mesh['box'=4,'grp'=8] {'grp'}, dimensions={0} | all-to-all | bytes 4194304 | tf_op jit(solution)/shard_map/all_to_all | solution.py:454
  177.6 1.3 copy.10
  (3 shorter events, 0.0 us)
Async XLA Ops:
  0.0 1.6 copy-start
  1.6 1.6 copy-start.1
  3.2 0.9 copy-start.6
  4.1 0.9 copy-start.8
  5.0 0.7 copy-start.17
  5.7 0.7 copy-start.19
  6.4 49.3 %copy-start.2 = (f32[1,16,32,1024]{3,2,1,0:T(8,128)S(1)}, f32[1,16,32,1024]{3,2,1,0:T(8,128)}, u32[]{:S(2)}) copy-start(f32[1,16,32,1024]{3,2,1,0:T(8,128)} %param.8) | copy-start | bytes 6291460
  6.4 49.3 %copy-start.18 = (s32[16]{0:T(128)S(1)}, s32[16]{0:T(128)}, u32[]{:S(2)}) copy-start(s32[16]{0:T(128)} %pos.3) | copy-start | bytes 196
  6.4 49.3 %copy-start.20 = (s32[16,1]{0,1:T(1,128)S(1)}, s32[16,1]{0,1:T(1,128)}, u32[]{:S(2)}) copy-start(s32[16,1]{0,1:T(1,128)} %param.14) | copy-start | bytes 196
  12.0 0.7 copy-start.5
  12.8 0.6 copy-start.13
  13.4 0.6 copy-start.14
  55.7 0.8 copy-start.9
  56.6 0.8 copy-start.10
  76.7 1.3 copy-start.3
  78.0 0.7 copy-start.7
  78.7 0.6 copy-start.15
  79.3 0.6 copy-start.16
  107.6 1.6 copy-start.4
  109.2 0.8 copy-start.11
  110.1 0.8 copy-start.12

commit v2 on v1

--- a/solution.py
+++ b/solution.py
@@ -13,6 +13,7 @@
 FACES, COARSE = 32, 8
 ROWS = FACES + COARSE
 OUTER = 4
+VMEM_BYTES = 60 * 1024 * 1024
 STEPS = ((-1, 0), (1, 0), (0, -1), (0, 1))
 HIGHEST = lax.Precision.HIGHEST
 
@@ -142,28 +143,28 @@
 
 
 def pack_kernel(count, pos, ref, phi, beta, coarse, pick, sent, up, down):
+    q = pl.program_id(0)
     half = coarse.shape[1]
-    wide = jnp.dot(
-        coarse[...].reshape(count * half, coarse.shape[2]), pick[...],
-        precision=HIGHEST, preferred_element_type=jnp.float32,
-    )
-    lane = lane_of((8, LANES))
-    row = lax.broadcasted_iota(jnp.int32, (8, LANES), 0)
-    meta = jnp.zeros((8, LANES), jnp.int32)
-    for q in range(count):
-        sent[q * ROWS + FACES : (q + 1) * ROWS, :] = folded(wide[q * half : (q + 1) * half])
-        meta = jnp.where((lane == q) & (row == 0), pos[q], meta)
-        meta = jnp.where((lane == q) & (row == 1), ref[q], meta)
-    sent[count * ROWS :, :] = meta.astype(jnp.float32)
-
-    def one(q, carry):
-        tile = mixed(1, faces(groups_of(phi[q])), faces(groups_of(beta[q])))
-        sent[pl.ds(pl.multiple_of(q * ROWS, 8), FACES), :] = tile
-        down[q] = mixed_row(1, 0, phi[q, 0:1, :], beta[q, 0:1, :])
-        up[q] = mixed_row(1, 1, phi[q, 31:32, :], beta[q, 31:32, :])
-        return carry
-
-    lax.fori_loop(0, count, one, 0)
+
+    @pl.when(q == 0)
+    def _():
+        wide = jnp.dot(
+            coarse[...].reshape(count * half, coarse.shape[2]), pick[...],
+            precision=HIGHEST, preferred_element_type=jnp.float32,
+        )
+        lane = lane_of((8, LANES))
+        row = lax.broadcasted_iota(jnp.int32, (8, LANES), 0)
+        meta = jnp.zeros((8, LANES), jnp.int32)
+        for s in range(count):
+            sent[s * ROWS + FACES : (s + 1) * ROWS, :] = folded(wide[s * half : (s + 1) * half])
+            meta = jnp.where((lane == s) & (row == 0), pos[s], meta)
+            meta = jnp.where((lane == s) & (row == 1), ref[s], meta)
+        sent[count * ROWS :, :] = meta.astype(jnp.float32)
+
+    tile = mixed(1, faces(groups_of(phi[0])), faces(groups_of(beta[0])))
+    sent[pl.ds(pl.multiple_of(q * ROWS, 8), FACES), :] = tile
+    down[0] = mixed_row(1, 0, phi[0, 0:1, :], beta[0, 0:1, :])
+    up[0] = mixed_row(1, 1, phi[0, 31:32, :], beta[0, 31:32, :])
 
 
 def exchange_kernel(n, slabs, sent, up, down, got, low, high, send, recv, x_send, x_recv, local):
@@ -255,7 +256,9 @@
             pltpu.SemaphoreType.DMA((1 + n // OUTER, n)), pltpu.SemaphoreType.DMA((n,)),
             pltpu.SemaphoreType.DMA((2,)), pltpu.SemaphoreType.DMA((2,)), pltpu.SemaphoreType.DMA,
         ],
-        compiler_params=pltpu.CompilerParams(collective_id=number, has_side_effects=True),
+        compiler_params=pltpu.CompilerParams(
+            collective_id=number, has_side_effects=True, vmem_limit_bytes=VMEM_BYTES
+        ),
         name="exchange",
     )(sent, up, down)
 
@@ -385,27 +388,37 @@
     groups = lax.axis_size("grp")
     slots = count * groups
     owner = new_owner[:, 0]
-    vmem = pl.BlockSpec(memory_space=pltpu.VMEM)
     smem = pl.BlockSpec(memory_space=pltpu.SMEM)
-    params = pltpu.CompilerParams(vmem_limit_bytes=48 * 1024 * 1024)
+    params = pltpu.CompilerParams(vmem_limit_bytes=VMEM_BYTES)
+    def own(*shape):
+        return pl.BlockSpec((1,) + shape, lambda q, *_: (q, 0, 0))
+
+    def full(*shape):
+        return pl.BlockSpec(shape, lambda q, *_: (0, 0, 0))
+
+    box = own(edge, area)
     sent, up, down = pl.pallas_call(
         functools.partial(pack_kernel, count),
-        out_shape=(struct(count * ROWS + 8, LANES), struct(count, 1, area), struct(count, 1, area)),
-        in_specs=[smem, smem, vmem, vmem, vmem, vmem],
-        out_specs=(vmem, vmem, vmem),
+        out_shape=(
+            struct(count * ROWS + 8, LANES), struct(count, 1, area), struct(count, 1, area)
+        ),
+        grid_spec=pltpu.PrefetchScalarGridSpec(
+            num_scalar_prefetch=2,
+            grid=(count,),
+            in_specs=[
+                box, box, full(*coarse.shape), pl.BlockSpec((area // 4, LANES), lambda q, *_: (0, 0))
+            ],
+            out_specs=[
+                pl.BlockSpec((count * ROWS + 8, LANES), lambda q, *_: (0, 0)), own(1, area),
+                own(1, area),
+            ],
+        ),
         compiler_params=params,
         name="pack",
     )(old_pos, refined, phi, beta, coarse, jnp.asarray(coarse_pick(edge // 2)))
     got, low, high = exchanged(0, sent, up, down)
     meta = got[:, count * ROWS : count * ROWS + 2, :count].astype(jnp.int32).reshape(2 * slots)
 
-    def own(*shape):
-        return pl.BlockSpec((1,) + shape, lambda q, *_: (q, 0, 0))
-
-    def full(*shape):
-        return pl.BlockSpec(shape, lambda q, *_: (0, 0, 0))
-
-    box = own(edge, area)
     middle, tile, up2, down2, coarse_tile, near, source = pl.pallas_call(
         functools.partial(first_kernel, count, slots),
         out_shape=(

time: 180 us -> 174 us (0.967)
  local copies, waits for them, and re-layouts: 17.9 us -> 1.99 us
  Pallas kernels: 108 us -> 118 us
    unnamed x43 -> x1, local copies, waits for them, and re-layouts: 17.8 us -> 1.32 us
    pallas_call x1, Pallas kernels: 5.66 us -> 13 us  [shards(): pl.pallas_call(functools.partial(pack_kernel, count), out_shape=(struct(c...]
    pallas_call x1, Pallas kernels: 14.3 us -> 16.8 us  [shards(): pl.pallas_call(second_kernel, out_shape=struct(groups * CAP, edge, area),...]
where the time goes in v2:
time: 174 us; the launch traced here: 173 us
  Pallas kernels  118 us (68%)
  blocking collectives  52.1 us (30%)
  local copies, waits for them, and re-layouts  1.99 us (1%)
    pallas_call x2, Pallas kernels, exchanged(): pl.pallas_call(functools.partial(exchange_kernel, n, slabs), out_shape=(s...  68.6 us
    all_to_all x1, blocking collectives, shards(): lax.all_to_all(ordered.reshape(groups, CAP, edge, area), 'grp', split_axi...  52.1 us
    pallas_call x1, Pallas kernels, shards(): pl.pallas_call(functools.partial(first_kernel, count, slots), out_shape=(...  19.5 us
    pallas_call x1, Pallas kernels, shards(): pl.pallas_call(second_kernel, out_shape=struct(groups * CAP, edge, area),...  16.8 us
    pallas_call x1, Pallas kernels, shards(): pl.pallas_call(functools.partial(pack_kernel, count), out_shape=(struct(c...  13 us

profile of v2, /device:TPU:0, one launch (start us, length us, event | category | flops | bytes accessed | tf_op | source)
XLA Modules:
  0.0 172.7 jit_solution(8771661864675823490)
XLA Ops:
  0.0 13.0 %pack.1 = (f32[648,128]{1,0:T(8,128)}, f32[16,1,1024]{2,1,0:T(1,128)}, f32[16,1,1024]{2,1,0:T(1,128)}) custom-call(s32[16]{0:T(128)} %pos.3, s32[16]{0:T(128)} %ref.1, f32[16,32,1024]{2,1,0:T(8,128)} %bitcast.11, f32[16,32,1024]{2,1,0:T(8,128)} %bitcast.8, f32[16,16,256]{2,1,0:T(8,128)} %bitcast.18, f32[256,128]{1,0:T(8,128)} %constant.2.clone.pick), custom_call_target="tpu_custom_call" | custom-call | tf_op jit(solution)/shard_map/pack/pallas_call | solution.py:400
  13.0 40.9 %exchange.2 = (f32[8,648,128]{2,1,0:T(8,128)}, f32[16,1,1024]{2,1,0:T(1,128)}, f32[16,1,1024]{2,1,0:T(1,128)}) custom-call(f32[648,128]{1,0:T(8,128)} %get-tuple-element.21.sent, f32[16,1,1024]{2,1,0:T(1,128)} %get-tuple-element.22.up, f32[16,1,1024]{2,1,0:T(1,128)} %get-tuple-element.23.down), custom_call_target="tpu_custom_call" | custom-call | tf_op jit(solution)/shard_map/exchange/pallas_call | solution.py:250
  53.9 0.8 slice_convert_fusion
  54.6 0.7 reshape.9.meta
  55.3 19.5 %colour0.1 = (f32[16,32,1024]{2,1,0:T(8,128)}, f32[512,128]{1,0:T(8,128)}, f32[16,1,1024]{2,1,0:T(1,128)}, f32[16,1,1024]{2,1,0:T(1,128)}, f32[16,32,128]{2,1,0:T(8,128)}, /*index=5*/s32[64]{0:T(128)}, s32[16]{0:T(128)}) custom-call(s32[256]{0:T(256)} %reshape.9.meta, s32[16]{0:T(128)} %pos.3, s32[16]{0:T(128)} %bitcast.19, f32[16,32,1024]{2,1,0:T(8,128)} %bitcast.12, ...), custom_call_target="tpu_custom_call" | custom-call | tf_op jit(solution)/shard_map/colour0/pallas_call | solution.py:422
  74.8 27.7 %exchange.3 = (f32[8,512,128]{2,1,0:T(8,128)}, f32[16,1,1024]{2,1,0:T(1,128)}, f32[16,1,1024]{2,1,0:T(1,128)}) custom-call(f32[512,128]{1,0:T(8,128)} %get-tuple-element.30.sent, f32[16,1,1024]{2,1,0:T(1,128)} %get-tuple-element.31.up, f32[16,1,1024]{2,1,0:T(1,128)} %get-tuple-element.32.down), custom_call_target="tpu_custom_call" | custom-call | tf_op jit(solution)/shard_map/exchange/pallas_call | solution.py:250
  102.5 16.8 %colour1.1 = f32[16,32,1024]{2,1,0:T(8,128)} custom-call(s32[64]{0:T(128)} %get-tuple-element.27.near, s32[16]{0:T(128)} %get-tuple-element.28.source, f32[16,32,1024]{2,1,0:T(8,128)} %get-tuple-element.29.phi, f32[16,32,1024]{2,1,0:T(8,128)} %bitcast.14, f32[16,32,1024]{2,1,0:T(8,128)} %bitcast.10, f32[128,32,128]{2,1,0:T(8,128)} %bitcast.17, ...), custom_call_target="tpu_custom_call" | custom-call | tf_op jit(solution)/shard_map/colour1/pallas_call | solution.py:452
  119.3 52.1 %all_to_all.5 = f32[8,2,32,1024]{3,2,1,0:T(8,128)S(1)} all-to-all(f32[8,2,32,1024]{3,2,1,0:T(8,128)} %bitcast.16), channel_id=1, replica_groups=mesh['box'=4,'grp'=8] {'grp'}, dimensions={0} | all-to-all | bytes 4194304 | tf_op jit(solution)/shard_map/all_to_all | solution.py:467
  171.4 1.3 copy.10

commit v3 on v2

--- a/solution.py
+++ b/solution.py
@@ -344,28 +344,63 @@
     tile[...] = mixed(0, faces(parts), faces(groups_of(beta[0])))
 
 
-def second_kernel(
-    near, source, phi, rhs, beta, got, low, high, coarse_tile, out
+def deliver_kernel(
+    n, near, source, phi, rhs, beta, got, low, high, coarse_tile, moved, ready, send, recv, local
 ):
-    q = source[pl.program_id(0)]
-
-    @pl.when(q < 0)
-    def _():
-        out[...] = jnp.zeros_like(out)
-
-    @pl.when(q >= 0)
-    def _():
+    me = lax.axis_index("grp")
+    barrier = pltpu.get_barrier_semaphore()
+    for i in range(1, n):
+        pl.semaphore_signal(
+            barrier, inc=1, device_id={"grp": (me + i) % n}, device_id_type=pl.DeviceIdType.MESH
+        )
+    pl.semaphore_wait(barrier, n - 1)
+    side, place = me // (n // 2), me % (n // 2)
+
+    def copy(mine, theirs, to):
+        return pltpu.make_async_remote_copy(
+            src_ref=ready.at[mine], dst_ref=moved.at[theirs], send_sem=send.at[mine],
+            recv_sem=recv.at[theirs], device_id={"grp": to}, device_id_type=pl.DeviceIdType.MESH,
+        )
+
+    def solve(mine):
+        q = source[mine]
+        box = jnp.maximum(q, 0)
         tiles = []
         for k in range(4):
-            slot = near[q * 4 + k]
+            slot = near[box * 4 + k]
             tiles.append(jnp.where(slot >= 0, got[jnp.maximum(slot, 0)], 0.0))
         ghost = swapped(tiles)
-        phi_x, beta_x = halo_rows(low[0], high[0])
+        phi_x, beta_x = halo_rows(low[box], high[box])
         parts = half_sweep(
-            1, phi[0], rhs[0], beta[0], ghost + coarse_tile[0], paired(ghost, 0), phi_x, beta_x
+            1, phi[box], rhs[box], beta[box], ghost + coarse_tile[box], paired(ghost, 0),
+            phi_x, beta_x,
         )
         for g, part in enumerate(parts):
-            out[0, :, LANES * g : LANES * (g + 1)] = part
+            ready[mine, :, LANES * g : LANES * (g + 1)] = jnp.where(q >= 0, part, 0.0)
+
+    def one(t, carry):
+        i, c = t // CAP, t % CAP
+        far = (1 - side) * (n // 2) + (place + i) % (n // 2)
+        close = side * (n // 2) + (place + i + 1) % (n // 2)
+        to = jnp.where(i < n // 2, far, close)
+        mine = to * CAP + c
+        solve(mine)
+        pl.when(i < n - 1)(lambda: copy(mine, me * CAP + c, to).start())
+        return carry
+
+    lax.fori_loop(0, n * CAP, one, 0)
+    own = [
+        pltpu.make_async_copy(ready.at[me * CAP + c], moved.at[me * CAP + c], local.at[c])
+        for c in range(CAP)
+    ]
+    for each in own:
+        each.start()
+    for i in range(1, n):
+        other = (me + i) % n
+        for c in range(CAP):
+            copy(other * CAP + c, other * CAP + c, other).wait()
+    for each in own:
+        each.wait()
 
 
 def coarse_pick(half):
@@ -444,30 +479,23 @@
     )(meta, old_pos, owner, phi, rhs, beta, got, low, high)
     got2, low2, high2 = exchanged(1, tile, up2, down2)
 
-    def at(*shape):
-        return pl.BlockSpec(
-            (1,) + shape, lambda r, near, source: (jnp.maximum(source[r], 0), 0, 0)
-        )
-
-    ordered = pl.pallas_call(
-        second_kernel,
+    vmem = pl.BlockSpec(memory_space=pltpu.VMEM)
+    moved = pl.pallas_call(
+        functools.partial(deliver_kernel, groups),
         out_shape=struct(groups * CAP, edge, area),
-        grid_spec=pltpu.PrefetchScalarGridSpec(
-            num_scalar_prefetch=2,
-            grid=(groups * CAP,),
-            in_specs=[
-                at(edge, area), at(edge, area), at(edge, area), full(slots, edge, LANES),
-                at(1, area), at(1, area), at(edge, LANES),
-            ],
-            out_specs=box,
-        ),
-        compiler_params=params,
-        name="colour1",
+        in_specs=[smem, smem] + [vmem] * 7,
+        out_specs=pl.BlockSpec(memory_space=pl.ANY),
+        scratch_shapes=[
+            pltpu.VMEM((groups * CAP, edge, area), jnp.float32),
+            pltpu.SemaphoreType.DMA((groups * CAP,)), pltpu.SemaphoreType.DMA((groups * CAP,)),
+            pltpu.SemaphoreType.DMA((CAP,)),
+        ],
+        compiler_params=pltpu.CompilerParams(
+            collective_id=2, has_side_effects=True, vmem_limit_bytes=VMEM_BYTES
+        ),
+        name="deliver",
     )(near, source, middle, rhs, beta, got2.reshape(slots, edge, LANES), low2, high2, coarse_tile)
-    moved = lax.all_to_all(
-        ordered.reshape(groups, CAP, edge, area), "grp", split_axis=0, concat_axis=0, tiled=True
-    )
-    return moved.reshape(groups * CAP, edge, area)[None]
+    return moved[None]
 
 
 def solution(mesh):

time: 174 us -> 162 us (0.931)
  blocking collectives: 52.1 us -> 0 us
  Pallas kernels: 118 us -> 156 us
  local copies, waits for them, and re-layouts: 1.99 us -> 3.83 us
    all_to_all x1 -> x0, blocking collectives: 52.1 us -> none  [shards(): lax.all_to_all(ordered.reshape(groups, CAP, edge, area), 'grp', split_axi...]
    pallas_call x1, Pallas kernels: 16.8 us -> 55 us  [shards(): pl.pallas_call(functools.partial(deliver_kernel, groups), out_shape=struc...]
    unnamed x1, local copies, waits for them, and re-layouts: 1.32 us -> 3.16 us
where the time goes in v3:
time: 162 us; the launch traced here: 161 us
  Pallas kernels  156 us (96%)
  local copies, waits for them, and re-layouts  3.83 us (2%)
    pallas_call x2, Pallas kernels, exchanged(): pl.pallas_call(functools.partial(exchange_kernel, n, slabs), out_shape=(s...  68.6 us
    pallas_call x1, Pallas kernels, shards(): pl.pallas_call(functools.partial(deliver_kernel, groups), out_shape=struc...  55 us
    pallas_call x1, Pallas kernels, shards(): pl.pallas_call(functools.partial(first_kernel, count, slots), out_shape=(...  19.5 us
    pallas_call x1, Pallas kernels, shards(): pl.pallas_call(functools.partial(pack_kernel, count), out_shape=(struct(c...  13 us

profile of v3, /device:TPU:0, one launch (start us, length us, event | category | flops | bytes accessed | tf_op | source)
XLA Modules:
  0.0 160.7 jit_solution(6202275463112690542)
XLA Ops:
  0.0 13.0 %pack.1 = (f32[648,128]{1,0:T(8,128)}, f32[16,1,1024]{2,1,0:T(1,128)}, f32[16,1,1024]{2,1,0:T(1,128)}) custom-call(s32[16]{0:T(128)} %pos.3, s32[16]{0:T(128)} %ref.1, f32[16,32,1024]{2,1,0:T(8,128)} %bitcast.10, f32[16,32,1024]{2,1,0:T(8,128)} %bitcast.7, f32[16,16,256]{2,1,0:T(8,128)} %bitcast.16, f32[256,128]{1,0:T(8,128)} %constant.2.clone.pick), custom_call_target="tpu_custom_call" | custom-call | tf_op jit(solution)/shard_map/pack/pallas_call | solution.py:435
  13.0 40.9 %exchange.2 = (f32[8,648,128]{2,1,0:T(8,128)}, f32[16,1,1024]{2,1,0:T(1,128)}, f32[16,1,1024]{2,1,0:T(1,128)}) custom-call(f32[648,128]{1,0:T(8,128)} %get-tuple-element.21.sent, f32[16,1,1024]{2,1,0:T(1,128)} %get-tuple-element.22.up, f32[16,1,1024]{2,1,0:T(1,128)} %get-tuple-element.23.down), custom_call_target="tpu_custom_call" | custom-call | tf_op jit(solution)/shard_map/exchange/pallas_call | solution.py:250
  53.9 0.8 slice_convert_fusion
  54.6 0.7 reshape.6.meta
  55.3 19.5 %colour0.1 = (f32[16,32,1024]{2,1,0:T(8,128)}, f32[512,128]{1,0:T(8,128)}, f32[16,1,1024]{2,1,0:T(1,128)}, f32[16,1,1024]{2,1,0:T(1,128)}, f32[16,32,128]{2,1,0:T(8,128)}, /*index=5*/s32[64]{0:T(128)}, s32[16]{0:T(128)}) custom-call(s32[256]{0:T(256)} %reshape.6.meta, s32[16]{0:T(128)} %pos.3, s32[16]{0:T(128)} %bitcast.17, f32[16,32,1024]{2,1,0:T(8,128)} %bitcast.11, ...), custom_call_target="tpu_custom_call" | custom-call | tf_op jit(solution)/shard_map/colour0/pallas_call | solution.py:457
  74.8 27.7 %exchange.3 = (f32[8,512,128]{2,1,0:T(8,128)}, f32[16,1,1024]{2,1,0:T(1,128)}, f32[16,1,1024]{2,1,0:T(1,128)}) custom-call(f32[512,128]{1,0:T(8,128)} %get-tuple-element.30.sent, f32[16,1,1024]{2,1,0:T(1,128)} %get-tuple-element.31.up, f32[16,1,1024]{2,1,0:T(1,128)} %get-tuple-element.32.down), custom_call_target="tpu_custom_call" | custom-call | tf_op jit(solution)/shard_map/exchange/pallas_call | solution.py:250
  102.5 55.0 %deliver.1 = f32[16,32,1024]{2,1,0:T(8,128)} custom-call(s32[64]{0:T(128)} %get-tuple-element.27.near, s32[16]{0:T(128)} %get-tuple-element.28.source, f32[16,32,1024]{2,1,0:T(8,128)} %get-tuple-element.29.phi, f32[16,32,1024]{2,1,0:T(8,128)} %bitcast.13, f32[16,32,1024]{2,1,0:T(8,128)} %bitcast.9, f32[128,32,128]{2,1,0:T(8,128)} %bitcast.15, ...), custom_call_target="tpu_custom_call" | custom-call | tf_op jit(solution)/shard_map/deliver/pallas_call | solution.py:483
  157.5 3.2 %copy.10 = f32[1,16,32,1024]{3,2,1,0:T(8,128)} copy(f32[1,16,32,1024]{3,2,1,0:T(8,128)} %bitcast.14) | data formatting | bytes 4194304

commit v4 on v3

--- a/solution.py
+++ b/solution.py
@@ -13,6 +13,8 @@
 FACES, COARSE = 32, 8
 ROWS = FACES + COARSE
 OUTER = 4
+PARTS = 4
+BATCH = 4
 VMEM_BYTES = 60 * 1024 * 1024
 STEPS = ((-1, 0), (1, 0), (0, -1), (0, 1))
 HIGHEST = lax.Precision.HIGHEST
@@ -161,10 +163,11 @@
             meta = jnp.where((lane == s) & (row == 1), ref[s], meta)
         sent[count * ROWS :, :] = meta.astype(jnp.float32)
 
-    tile = mixed(1, faces(groups_of(phi[0])), faces(groups_of(beta[0])))
-    sent[pl.ds(pl.multiple_of(q * ROWS, 8), FACES), :] = tile
-    down[0] = mixed_row(1, 0, phi[0, 0:1, :], beta[0, 0:1, :])
-    up[0] = mixed_row(1, 1, phi[0, 31:32, :], beta[0, 31:32, :])
+    for b in range(BATCH):
+        tile = mixed(1, faces(groups_of(phi[b])), faces(groups_of(beta[b])))
+        sent[pl.ds(pl.multiple_of((q * BATCH + b) * ROWS, 8), FACES), :] = tile
+        down[b] = mixed_row(1, 0, phi[b, 0:1, :], beta[b, 0:1, :])
+        up[b] = mixed_row(1, 1, phi[b, 31:32, :], beta[b, 31:32, :])
 
 
 def exchange_kernel(n, slabs, sent, up, down, got, low, high, send, recv, x_send, x_recv, local):
@@ -190,15 +193,20 @@
         total = total + there.astype(jnp.int32)
     pl.semaphore_wait(barrier, total)
 
-    def copy(src, block, lane, to):
+    rows = sent.shape[0]
+    cuts = [rows * p // (8 * PARTS) * 8 for p in range(PARTS)] + [rows]
+
+    def copy(src, block, lane, to, p):
+        span = pl.ds(cuts[p], cuts[p + 1] - cuts[p])
         return pltpu.make_async_remote_copy(
-            src_ref=src, dst_ref=got.at[block], send_sem=send.at[lane, block],
-            recv_sem=recv.at[block], device_id=device(to), device_id_type=pl.DeviceIdType.MESH,
+            src_ref=sent.at[span] if src is None else got.at[src, span],
+            dst_ref=got.at[block, span], send_sem=send.at[lane, block, p],
+            recv_sem=recv.at[block, p], device_id=device(to), device_id_type=pl.DeviceIdType.MESH,
         )
 
-    def beside(block, src):
+    def beside(block, src, p):
         for i, to in enumerate(mates):
-            copy(src, block, 2 + i, to).start()
+            copy(src, block, 2 + i, to, p).start()
 
     def along_x(src, dst, lane, to):
         return pltpu.make_async_remote_copy(
@@ -206,40 +214,45 @@
             device_id={"box": to}, device_id_type=pl.DeviceIdType.MESH,
         )
 
-    pl.when(z < OUTER - 1)(lambda: copy(sent, me, 0, me + inner).start())
-    pl.when(z > 0)(lambda: copy(sent, me, 1, me - inner).start())
-    beside(me, sent)
+    for p in range(PARTS):
+        pl.when(z < OUTER - 1)(lambda: copy(None, me, 0, me + inner, p).start())
+        pl.when(z > 0)(lambda: copy(None, me, 1, me - inner, p).start())
+        beside(me, None, p)
     pl.when(slab < slabs - 1)(lambda: along_x(up, low, 0, slab + 1).start())
     pl.when(slab > 0)(lambda: along_x(down, high, 1, slab - 1).start())
     own = pltpu.make_async_copy(sent, got.at[me], local)
     own.start()
     for s in range(1, OUTER):
-        @pl.when(z >= s)
-        def _(s=s):
-            block = me - s * inner
-            copy(got.at[block], block, 0, block).wait_recv()
-            pl.when(z < OUTER - 1)(lambda: copy(got.at[block], block, 0, me + inner).start())
-            beside(block, got.at[block])
-
-        @pl.when(z + s < OUTER)
-        def _(s=s):
-            block = me + s * inner
-            copy(got.at[block], block, 1, block).wait_recv()
-            pl.when(z > 0)(lambda: copy(got.at[block], block, 1, me - inner).start())
-            beside(block, got.at[block])
+        for p in range(PARTS):
+            @pl.when(z >= s)
+            def _(s=s, p=p):
+                block = me - s * inner
+                copy(block, block, 0, block, p).wait_recv()
+                pl.when(z < OUTER - 1)(lambda: copy(block, block, 0, me + inner, p).start())
+                beside(block, block, p)
+
+            @pl.when(z + s < OUTER)
+            def _(s=s, p=p):
+                block = me + s * inner
+                copy(block, block, 1, block, p).wait_recv()
+                pl.when(z > 0)(lambda: copy(block, block, 1, me - inner, p).start())
+                beside(block, block, p)
     for level in range(OUTER):
         for i, to in enumerate(mates):
             block = level * inner + (y + i + 1) % inner
-            copy(got.at[block], block, 2, to).wait_recv()
+            for p in range(PARTS):
+                copy(block, block, 2, to, p).wait_recv()
     own.wait()
     pl.when(slab > 0)(lambda: along_x(up, low, 0, slab - 1).wait_recv())
     pl.when(slab < slabs - 1)(lambda: along_x(down, high, 1, slab + 1).wait_recv())
     for level in range(OUTER):
         block = level * inner + y
-        pl.when((z < OUTER - 1) & (level <= z))(lambda: copy(sent, block, 0, me + inner).wait_send())
-        pl.when((z > 0) & (level >= z))(lambda: copy(sent, block, 1, me - inner).wait_send())
-        for i, to in enumerate(mates):
-            copy(sent, block, 2 + i, to).wait_send()
+        for p in range(PARTS):
+            up_link, down_link = (z < OUTER - 1) & (level <= z), (z > 0) & (level >= z)
+            pl.when(up_link)(lambda: copy(None, block, 0, me + inner, p).wait_send())
+            pl.when(down_link)(lambda: copy(None, block, 1, me - inner, p).wait_send())
+            for i, to in enumerate(mates):
+                copy(None, block, 2 + i, to, p).wait_send()
     pl.when(slab < slabs - 1)(lambda: along_x(up, low, 0, slab + 1).wait_send())
     pl.when(slab > 0)(lambda: along_x(down, high, 1, slab - 1).wait_send())
 
@@ -253,7 +266,8 @@
         in_specs=[anywhere] * 3,
         out_specs=(anywhere,) * 3,
         scratch_shapes=[
-            pltpu.SemaphoreType.DMA((1 + n // OUTER, n)), pltpu.SemaphoreType.DMA((n,)),
+            pltpu.SemaphoreType.DMA((1 + n // OUTER, n, PARTS)),
+            pltpu.SemaphoreType.DMA((n, PARTS)),
             pltpu.SemaphoreType.DMA((2,)), pltpu.SemaphoreType.DMA((2,)), pltpu.SemaphoreType.DMA,
         ],
         compiler_params=pltpu.CompilerParams(
@@ -428,6 +442,9 @@
     def own(*shape):
         return pl.BlockSpec((1,) + shape, lambda q, *_: (q, 0, 0))
 
+    def batch(*shape):
+        return pl.BlockSpec((BATCH,) + shape, lambda q, *_: (q, 0, 0))
+
     def full(*shape):
         return pl.BlockSpec(shape, lambda q, *_: (0, 0, 0))
 
@@ -439,13 +456,13 @@
         ),
         grid_spec=pltpu.PrefetchScalarGridSpec(
             num_scalar_prefetch=2,
-            grid=(count,),
+            grid=(count // BATCH,),
             in_specs=[
-                box, box, full(*coarse.shape), pl.BlockSpec((area // 4, LANES), lambda q, *_: (0, 0))
+                batch(edge, area), batch(edge, area), full(*coarse.shape), pl.BlockSpec((area // 4, LANES), lambda q, *_: (0, 0))
             ],
             out_specs=[
-                pl.BlockSpec((count * ROWS + 8, LANES), lambda q, *_: (0, 0)), own(1, area),
-                own(1, area),
+                pl.BlockSpec((count * ROWS + 8, LANES), lambda q, *_: (0, 0)), batch(1, area),
+                batch(1, area),
             ],
         ),
         compiler_params=params,

time: 162 us -> 150 us (0.926)
  Pallas kernels: 156 us -> 145 us
    pallas_call x2, Pallas kernels: 68.6 us -> 62.1 us  [exchanged(): pl.pallas_call(functools.partial(exchange_kernel, n, slabs), out_shape=(s...]
    pallas_call x1, Pallas kernels: 13 us -> 7.45 us  [shards(): pl.pallas_call(functools.partial(pack_kernel, count), out_shape=(struct(c...]
where the time goes in v4:
time: 150 us
  Pallas kernels  145 us (97%)
  local copies, waits for them, and re-layouts  3.83 us (3%)
    pallas_call x2, Pallas kernels, exchanged(): pl.pallas_call(functools.partial(exchange_kernel, n, slabs), out_shape=(s...  62.1 us
    pallas_call x1, Pallas kernels, shards(): pl.pallas_call(functools.partial(deliver_kernel, groups), out_shape=struc...  56 us
    pallas_call x1, Pallas kernels, shards(): pl.pallas_call(functools.partial(first_kernel, count, slots), out_shape=(...  19.5 us
    pallas_call x1, Pallas kernels, shards(): pl.pallas_call(functools.partial(pack_kernel, count), out_shape=(struct(c...  7.45 us
    unnamed x1, local copies, waits for them, and re-layouts  3.16 us

profile of v4, /device:TPU:0, one launch (start us, length us, event | category | flops | bytes accessed | tf_op | source)
XLA Modules:
  0.0 149.7 jit_solution(1512851331989257740)
XLA Ops:
  0.0 7.5 %pack.1 = (f32[648,128]{1,0:T(8,128)}, f32[16,1,1024]{2,1,0:T(1,128)}, f32[16,1,1024]{2,1,0:T(1,128)}) custom-call(s32[16]{0:T(128)} %pos.3, s32[16]{0:T(128)} %ref.1, f32[16,32,1024]{2,1,0:T(8,128)} %bitcast.10, f32[16,32,1024]{2,1,0:T(8,128)} %bitcast.7, f32[16,16,256]{2,1,0:T(8,128)} %bitcast.16, f32[256,128]{1,0:T(8,128)} %constant.2.clone.pick), custom_call_target="tpu_custom_call" | custom-call | tf_op jit(solution)/shard_map/pack/pallas_call | solution.py:452
  7.5 35.5 %exchange.2 = (f32[8,648,128]{2,1,0:T(8,128)}, f32[16,1,1024]{2,1,0:T(1,128)}, f32[16,1,1024]{2,1,0:T(1,128)}) custom-call(f32[648,128]{1,0:T(8,128)} %get-tuple-element.21.sent, f32[16,1,1024]{2,1,0:T(1,128)} %get-tuple-element.22.up, f32[16,1,1024]{2,1,0:T(1,128)} %get-tuple-element.23.down), custom_call_target="tpu_custom_call" | custom-call | tf_op jit(solution)/shard_map/exchange/pallas_call | solution.py:263
  43.0 0.8 slice_convert_fusion
  43.7 0.7 reshape.6.meta
  44.4 19.5 %colour0.1 = (f32[16,32,1024]{2,1,0:T(8,128)}, f32[512,128]{1,0:T(8,128)}, f32[16,1,1024]{2,1,0:T(1,128)}, f32[16,1,1024]{2,1,0:T(1,128)}, f32[16,32,128]{2,1,0:T(8,128)}, /*index=5*/s32[64]{0:T(128)}, s32[16]{0:T(128)}) custom-call(s32[256]{0:T(256)} %reshape.6.meta, s32[16]{0:T(128)} %pos.3, s32[16]{0:T(128)} %bitcast.17, f32[16,32,1024]{2,1,0:T(8,128)} %bitcast.11, ...), custom_call_target="tpu_custom_call" | custom-call | tf_op jit(solution)/shard_map/colour0/pallas_call | solution.py:474
  63.9 26.6 %exchange.3 = (f32[8,512,128]{2,1,0:T(8,128)}, f32[16,1,1024]{2,1,0:T(1,128)}, f32[16,1,1024]{2,1,0:T(1,128)}) custom-call(f32[512,128]{1,0:T(8,128)} %get-tuple-element.30.sent, f32[16,1,1024]{2,1,0:T(1,128)} %get-tuple-element.31.up, f32[16,1,1024]{2,1,0:T(1,128)} %get-tuple-element.32.down), custom_call_target="tpu_custom_call" | custom-call | tf_op jit(solution)/shard_map/exchange/pallas_call | solution.py:263
  90.5 56.0 %deliver.1 = f32[16,32,1024]{2,1,0:T(8,128)} custom-call(s32[64]{0:T(128)} %get-tuple-element.27.near, s32[16]{0:T(128)} %get-tuple-element.28.source, f32[16,32,1024]{2,1,0:T(8,128)} %get-tuple-element.29.phi, f32[16,32,1024]{2,1,0:T(8,128)} %bitcast.13, f32[16,32,1024]{2,1,0:T(8,128)} %bitcast.9, f32[128,32,128]{2,1,0:T(8,128)} %bitcast.15, ...), custom_call_target="tpu_custom_call" | custom-call | tf_op jit(solution)/shard_map/deliver/pallas_call | solution.py:500
  146.5 3.2 %copy.10 = f32[1,16,32,1024]{3,2,1,0:T(8,128)} copy(f32[1,16,32,1024]{3,2,1,0:T(8,128)} %bitcast.14) | data formatting | bytes 4194304

commit v5 on v4

--- a/solution.py
+++ b/solution.py
@@ -328,34 +328,41 @@
 
         lax.fori_loop(0, count, give, 0)
 
-    here = pos[q]
-    row, col = lax.div(here, count), lax.rem(here, count)
-    fine_tiles, under = [], []
-    for k, (dy, dz) in enumerate(STEPS):
-        y, z = row + dy, col + dz
-        inside = (y >= 0) & (y < groups) & (z >= 0) & (z < count)
-        spot = jnp.where(inside, y * count + z, 0)
-        fine = inside & refined_at(spot)
-        slot = holder[spot]
-        near[q * 4 + k] = jnp.where(fine, slot, -1)
-        fine_tiles.append(jnp.where(fine, rows(slot, 0, FACES), 0.0))
-        under.append(jnp.where(inside & jnp.logical_not(fine), rows(spot, FACES, COARSE), 0.0))
-    for i, narrow in enumerate(unfolded(swapped(under))):
-        for odd in range(2):
-            wide[pl.ds(2 * COARSE * i + odd, COARSE, stride=2), :] = narrow
-    coarse_ghost = wide[...]
-    coarse_tile[0] = coarse_ghost
-    ghost = swapped(fine_tiles)
-    phi_x, beta_x = halo_rows(low[0], high[0])
-    parts = half_sweep(
-        0, phi[0], rhs[0], beta[0], ghost + coarse_ghost, paired(ghost, 0), phi_x, beta_x
-    )
-    for g, part in enumerate(parts):
-        cut = slice(LANES * g, LANES * (g + 1))
-        out[0, :, cut] = part
-        down[0, :, cut] = mixed_row(0, 0, part[0:1], beta[0, 0:1, cut])
-        up[0, :, cut] = mixed_row(0, 1, part[31:32], beta[0, 31:32, cut])
-    tile[...] = mixed(0, faces(parts), faces(groups_of(beta[0])))
+    def one(b, carry):
+        box = q * BATCH + b
+        here = pos[box]
+        row, col = lax.div(here, count), lax.rem(here, count)
+        fine_tiles, under = [], []
+        for k, (dy, dz) in enumerate(STEPS):
+            y, z = row + dy, col + dz
+            inside = (y >= 0) & (y < groups) & (z >= 0) & (z < count)
+            spot = jnp.where(inside, y * count + z, 0)
+            fine = inside & refined_at(spot)
+            slot = holder[spot]
+            near[box * 4 + k] = jnp.where(fine, slot, -1)
+            fine_tiles.append(jnp.where(fine, rows(slot, 0, FACES), 0.0))
+            under.append(jnp.where(inside & jnp.logical_not(fine), rows(spot, FACES, COARSE), 0.0))
+        for i, narrow in enumerate(unfolded(swapped(under))):
+            for odd in range(2):
+                wide[pl.ds(2 * COARSE * i + odd, COARSE, stride=2), :] = narrow
+        coarse_ghost = wide[...]
+        coarse_tile[b] = coarse_ghost
+        ghost = swapped(fine_tiles)
+        phi_x, beta_x = halo_rows(low[b], high[b])
+        parts = half_sweep(
+            0, phi[b], rhs[b], beta[b], ghost + coarse_ghost, paired(ghost, 0), phi_x, beta_x
+        )
+        for g, part in enumerate(parts):
+            cut = slice(LANES * g, LANES * (g + 1))
+            out[b, :, cut] = part
+            down[b, :, cut] = mixed_row(0, 0, part[0:1], beta[b, 0:1, cut])
+            up[b, :, cut] = mixed_row(0, 1, part[31:32], beta[b, 31:32, cut])
+        tile[pl.ds(pl.multiple_of(b * FACES, 8), FACES), :] = mixed(
+            0, faces(parts), faces(groups_of(beta[b]))
+        )
+        return carry
+
+    lax.fori_loop(0, BATCH, one, 0)
 
 
 def deliver_kernel(
@@ -448,7 +455,6 @@
     def full(*shape):
         return pl.BlockSpec(shape, lambda q, *_: (0, 0, 0))
 
-    box = own(edge, area)
     sent, up, down = pl.pallas_call(
         functools.partial(pack_kernel, count),
         out_shape=(
@@ -480,11 +486,11 @@
         ),
         grid_spec=pltpu.PrefetchScalarGridSpec(
             num_scalar_prefetch=3,
-            grid=(count,),
-            in_specs=[box, box, box, full(groups, count * ROWS + 8, LANES), own(1, area), own(1, area)],
+            grid=(count // BATCH,),
+            in_specs=[batch(edge, area)] * 3 + [full(groups, count * ROWS + 8, LANES), batch(1, area), batch(1, area)],
             out_specs=[
-                box, pl.BlockSpec((edge, LANES), lambda q, *_: (q, 0)), own(1, area), own(1, area),
-                own(edge, LANES), smem, smem,
+                batch(edge, area), pl.BlockSpec((BATCH * edge, LANES), lambda q, *_: (q, 0)), batch(1, area), batch(1, area),
+                batch(edge, LANES), smem, smem,
             ],
             scratch_shapes=[
                 pltpu.SMEM((slots,), jnp.int32), pltpu.SMEM((groups,), jnp.int32),

time: 150 us -> 150 us (level)
  no operation moved by 1% of the time
where the time goes in v5:
time: 150 us
  Pallas kernels  145 us (97%)
  local copies, waits for them, and re-layouts  3.83 us (3%)
    pallas_call x2, Pallas kernels, exchanged(): pl.pallas_call(functools.partial(exchange_kernel, n, slabs), out_shape=(s...  62.1 us
    pallas_call x1, Pallas kernels, shards(): pl.pallas_call(functools.partial(deliver_kernel, groups), out_shape=struc...  56 us
    pallas_call x1, Pallas kernels, shards(): pl.pallas_call(functools.partial(first_kernel, count, slots), out_shape=(...  19.4 us
    pallas_call x1, Pallas kernels, shards(): pl.pallas_call(functools.partial(pack_kernel, count), out_shape=(struct(c...  7.45 us
    unnamed x1, local copies, waits for them, and re-layouts  3.16 us

profile of v5, /device:TPU:0, one launch (start us, length us, event | category | flops | bytes accessed | tf_op | source)
XLA Modules:
  0.0 149.7 jit_solution(5334094085698959330)
XLA Ops:
  0.0 7.5 %pack.1 = (f32[648,128]{1,0:T(8,128)}, f32[16,1,1024]{2,1,0:T(1,128)}, f32[16,1,1024]{2,1,0:T(1,128)}) custom-call(s32[16]{0:T(128)} %pos.3, s32[16]{0:T(128)} %ref.1, f32[16,32,1024]{2,1,0:T(8,128)} %bitcast.10, f32[16,32,1024]{2,1,0:T(8,128)} %bitcast.7, f32[16,16,256]{2,1,0:T(8,128)} %bitcast.16, f32[256,128]{1,0:T(8,128)} %constant.2.clone.pick), custom_call_target="tpu_custom_call" | custom-call | tf_op jit(solution)/shard_map/pack/pallas_call | solution.py:458
  7.5 35.5 %exchange.2 = (f32[8,648,128]{2,1,0:T(8,128)}, f32[16,1,1024]{2,1,0:T(1,128)}, f32[16,1,1024]{2,1,0:T(1,128)}) custom-call(f32[648,128]{1,0:T(8,128)} %get-tuple-element.21.sent, f32[16,1,1024]{2,1,0:T(1,128)} %get-tuple-element.22.up, f32[16,1,1024]{2,1,0:T(1,128)} %get-tuple-element.23.down), custom_call_target="tpu_custom_call" | custom-call | tf_op jit(solution)/shard_map/exchange/pallas_call | solution.py:263
  43.0 0.8 slice_convert_fusion
  43.7 0.7 reshape.6.meta
  44.4 19.4 %colour0.1 = (f32[16,32,1024]{2,1,0:T(8,128)}, f32[512,128]{1,0:T(8,128)}, f32[16,1,1024]{2,1,0:T(1,128)}, f32[16,1,1024]{2,1,0:T(1,128)}, f32[16,32,128]{2,1,0:T(8,128)}, /*index=5*/s32[64]{0:T(128)}, s32[16]{0:T(128)}) custom-call(s32[256]{0:T(256)} %reshape.6.meta, s32[16]{0:T(128)} %pos.3, s32[16]{0:T(128)} %bitcast.17, f32[16,32,1024]{2,1,0:T(8,128)} %bitcast.11, ...), custom_call_target="tpu_custom_call" | custom-call | tf_op jit(solution)/shard_map/colour0/pallas_call | solution.py:480
  63.9 26.6 %exchange.3 = (f32[8,512,128]{2,1,0:T(8,128)}, f32[16,1,1024]{2,1,0:T(1,128)}, f32[16,1,1024]{2,1,0:T(1,128)}) custom-call(f32[512,128]{1,0:T(8,128)} %get-tuple-element.30.sent, f32[16,1,1024]{2,1,0:T(1,128)} %get-tuple-element.31.up, f32[16,1,1024]{2,1,0:T(1,128)} %get-tuple-element.32.down), custom_call_target="tpu_custom_call" | custom-call | tf_op jit(solution)/shard_map/exchange/pallas_call | solution.py:263
  90.5 56.0 %deliver.1 = f32[16,32,1024]{2,1,0:T(8,128)} custom-call(s32[64]{0:T(128)} %get-tuple-element.27.near, s32[16]{0:T(128)} %get-tuple-element.28.source, f32[16,32,1024]{2,1,0:T(8,128)} %get-tuple-element.29.phi, f32[16,32,1024]{2,1,0:T(8,128)} %bitcast.13, f32[16,32,1024]{2,1,0:T(8,128)} %bitcast.9, f32[128,32,128]{2,1,0:T(8,128)} %bitcast.15, ...), custom_call_target="tpu_custom_call" | custom-call | tf_op jit(solution)/shard_map/deliver/pallas_call | solution.py:506
  146.5 3.2 %copy.10 = f32[1,16,32,1024]{3,2,1,0:T(8,128)} copy(f32[1,16,32,1024]{3,2,1,0:T(8,128)} %bitcast.14) | data formatting | bytes 4194304
